TPU v7x, 768 devices: a whole 4x8x12 slice. The times are simulated.
768 devices in a mesh: dom: 96 (over z, x, core), sub: 8 (over y).
Axes of the slice: x: 4, y: 8, z: 12, core: 2. Of those that a mesh axis runs over, the one named last changes fastest.
Arguments:
- feats: bfloat16 [1572864, 128], P(('dom', 'sub')), may hold values from -6 to 6
- stale: bfloat16 [1572864, 128], P(('dom', 'sub')), may hold values from -6 to 6
- weight: bfloat16 [128, 128], replicated, may hold values from -0.5 to 0.5
- cotangent: bfloat16 [1572864, 128], P(('dom', 'sub')), may hold values from -6 to 6
- send_sub: int32 [6144, 64], P(('dom', 'sub')), may hold values from 0 to 2047
- send_dom: int32 [73728, 2], P(('dom', 'sub')), may hold values from 0 to 2047
- tile_index: int32 [768, 2, 48], P(('dom', 'sub')), may hold values from 0 to 21, as said below
- tile_count: int32 [768], P(('dom', 'sub')), may hold values from 22 to 48
- tile_values: bfloat16 [36864, 128, 128], P(('dom', 'sub')), may hold values from -0.3125 to 0.3125
Outputs:
- hidden_out: bfloat16 [1572864, 128], P(('dom', 'sub'))
- weight_grad: float32 [128, 128], replicated
- feat_grad: bfloat16 [1572864, 128], P(('dom', 'sub'))
Inputs may be any that keep to these rules, and one draw needn't show every extreme that they name: `tile_index`: slots 6 to 21 have row blocks 0 to 15 in order and column blocks 0 to 15 in order; slot t < 6 has column block 16 + t.
All inputs are finite; a program needn't handle non-finite values.
Results may differ from a plain program's by a relative error of at most 0.007.
Values may be sent and summed in bfloat16 or wider, within the bound.
A program may use at most 32 MiB of HBM per device.

v0:
```python
import jax
import jax.numpy as jnp
from jax import lax
from jax.sharding import PartitionSpec as P


def on_device(
    feats, stale, weight, cotangent, send_sub, send_dom, tile_index, tile_count, tile_values
):
    rows_dev, feat_width = feats.shape
    tile_size = tile_values.shape[1]
    tile_slots = tile_values.shape[0]
    row_blocks = rows_dev // tile_size
    sub_peers, sub_slots = send_sub.shape
    dom_peers, dom_slots = send_dom.shape
    sub_total = sub_peers * sub_slots
    halo_rows = sub_total + dom_peers * dom_slots
    halo_blocks = (halo_rows + tile_size - 1) // tile_size
    col_blocks = row_blocks + halo_blocks
    spare_rows = col_blocks * tile_size - rows_dev - halo_rows
    live_mask = jnp.arange(tile_slots) < tile_count[0]
    masked = jnp.where(live_mask[:, None, None], tile_values, jnp.zeros_like(tile_values))
    row_pick = tile_index[0, 0]
    col_pick = tile_index[0, 1]
    row_onehot = (row_pick[None, :] == jnp.arange(row_blocks)[:, None]).astype(jnp.float32)
    col_onehot = (col_pick[None, :] == jnp.arange(col_blocks)[:, None]).astype(jnp.float32)
    sub_rows = stale[send_sub.reshape(-1)].reshape(sub_peers, sub_slots, feat_width)
    dom_rows = stale[send_dom.reshape(-1)].reshape(dom_peers, dom_slots, feat_width)
    halo_sub = lax.all_to_all(sub_rows, "sub", split_axis=0, concat_axis=0, tiled=True)
    halo_dom = lax.all_to_all(dom_rows, "dom", split_axis=0, concat_axis=0, tiled=True)
    halo_cols = jnp.concatenate(
        [
            halo_sub.reshape(-1, feat_width),
            halo_dom.reshape(-1, feat_width),
            jnp.zeros((spare_rows, feat_width), jnp.bfloat16),
        ],
        axis=0,
    )
    all_blocks = jnp.concatenate([feats, halo_cols], axis=0).reshape(
        col_blocks, tile_size, feat_width
    )
    products = jnp.einsum(
        "tij,tjf->tif", masked, all_blocks[col_pick], preferred_element_type=jnp.float32
    )
    summed = jnp.einsum("rt,tif->rif", row_onehot, products, precision=lax.Precision.HIGHEST)
    aggregated = summed.reshape(rows_dev, feat_width).astype(jnp.bfloat16)
    pre_act = jnp.dot(aggregated, weight, preferred_element_type=jnp.float32)
    hidden_out = jax.nn.silu(pre_act).astype(jnp.bfloat16)
    gate_sig = jax.nn.sigmoid(pre_act)
    grad_z = (cotangent.astype(jnp.float32) * gate_sig * (1.0 + pre_act * (1.0 - gate_sig))).astype(
        jnp.bfloat16
    )
    weight_part = lax.dot_general(
        aggregated, grad_z, (((0,), (0,)), ((), ())), preferred_element_type=jnp.float32
    )
    weight_sum = lax.psum(weight_part, ("dom", "sub"))
    node_total = rows_dev * lax.axis_size("dom") * lax.axis_size("sub")
    weight_grad = weight_sum / jnp.sqrt(jnp.float32(node_total))
    grad_agg = lax.dot_general(
        grad_z, weight, (((1,), (1,)), ((), ())), preferred_element_type=jnp.float32
    ).astype(jnp.bfloat16)
    grad_blocks = grad_agg.reshape(row_blocks, tile_size, feat_width)[row_pick]
    back_terms = jnp.einsum("tji,tjf->tif", masked, grad_blocks, preferred_element_type=jnp.float32)
    grad_columns = jnp.einsum(
        "ct,tif->cif", col_onehot, back_terms, precision=lax.Precision.HIGHEST
    )
    grad_columns = grad_columns.reshape(col_blocks * tile_size, feat_width)
    own_grad = grad_columns[:rows_dev]
    sub_back = grad_columns[rows_dev : rows_dev + sub_total].reshape(
        sub_peers, sub_slots, feat_width
    )
    dom_back = grad_columns[rows_dev + sub_total : rows_dev + halo_rows].reshape(
        dom_peers, dom_slots, feat_width
    )
    return_sub = lax.all_to_all(
        sub_back.astype(jnp.bfloat16), "sub", split_axis=0, concat_axis=0, tiled=True
    ).astype(sub_back.dtype)
    return_dom = lax.all_to_all(dom_back, "dom", split_axis=0, concat_axis=0, tiled=True)
    grad_total = own_grad.at[send_sub.reshape(-1)].add(return_sub.reshape(-1, feat_width))
    grad_total = grad_total.at[send_dom.reshape(-1)].add(return_dom.reshape(-1, feat_width))
    return (hidden_out, weight_grad, grad_total.astype(jnp.bfloat16))


def solution(mesh):
    return jax.shard_map(
        on_device,
        mesh=mesh,
        in_specs=(
            P(("dom", "sub"), None),
            P(("dom", "sub"), None),
            P(),
            P(("dom", "sub"), None),
            P(("dom", "sub"), None),
            P(("dom", "sub"), None),
            P(("dom", "sub"), None, None),
            P(("dom", "sub")),
            P(("dom", "sub"), None, None),
        ),
        out_specs=(P(("dom", "sub"), None), P(), P(("dom", "sub"), None)),
        check_vma=False,
    )
```

profile of v0, /device:TPU:1, one launch (start us, length us, event | category | flops | bytes accessed | tf_op | source)
XLA Modules:
  0.0 561.7 jit_solution(9181749665291780081)
XLA Ops:
  7.2 0.9 copy.12
  8.2 1.4 gather_fusion.1
  9.6 20.0 %all-to-all-start.1 = ((bf16[96,2,128]{2,1,0:T(2,128)(2,1)}), bf16[96,2,128]{2,1,0:T(2,128)(2,1)S(1)}, u32[]{:S(2)}, u32[]{:S(2)}) async-start(bf16[96,2,128]{2,1,0:T(2,128)(2,1)} %bitcast.7), calls=%async_computation.1 | async-start | bytes 98304 | tf_op jit(solution)/shard_map/all_to_all | solution.py:30
  29.7 0.8 fusion.18
  30.4 0.8 reshape.172
  31.9 1.9 gather_fusion
  33.8 8.1 %all-to-all-done.1 = bf16[96,2,128]{2,1,0:T(2,128)(2,1)S(1)} async-done(((bf16[96,2,128]{2,1,0:T(2,128)(2,1)}), bf16[96,2,128]{2,1,0:T(2,128)(2,1)S(1)}, u32[]{:S(2)}, u32[]{:S(2)}) %all-to-all-start.1) | async-done | bytes 49184 | tf_op jit(solution)/shard_map/all_to_all | solution.py:30
  41.9 6.8 %all-to-all-start = ((bf16[8,64,128]{2,1,0:T(8,128)(2,1)}), bf16[8,64,128]{2,1,0:T(8,128)(2,1)S(1)}, u32[]{:S(2)}, u32[]{:S(2)}) async-start(bf16[8,64,128]{2,1,0:T(8,128)(2,1)} %bitcast.4), calls=%async_computation | async-start | bytes 262144 | tf_op jit(solution)/shard_map/all_to_all | solution.py:29
  48.8 7.9 %all-to-all-done = bf16[8,64,128]{2,1,0:T(8,128)(2,1)S(1)} async-done(((bf16[8,64,128]{2,1,0:T(8,128)(2,1)}), bf16[8,64,128]{2,1,0:T(8,128)(2,1)S(1)}, u32[]{:S(2)}, u32[]{:S(2)}) %all-to-all-start) | async-done | bytes 131104 | tf_op jit(solution)/shard_map/all_to_all | solution.py:29
  56.7 0.4 maximum_maximum_fusion
  57.1 2.0 gather_fusion.2
  59.1 2.0 fusion.8
  61.2 2.9 fusion.4
  64.3 1.5 multiply_convert_fusion
  65.8 0.8 copy-done.2
  66.5 0.3 convolution_convert_fusion
  66.8 2.0 gather_fusion.3
  68.8 2.2 fusion.7
  71.0 3.0 fusion
  74.0 0.7 copy.15
  74.7 3.4 all-to-all-start.2
  78.0 0.3 copy.16
  78.3 0.6 slice.36
  79.0 7.0 %all-to-all-done.2 = bf16[8,64,128]{2,1,0:T(8,128)(2,1)S(1)} async-done(((bf16[8,64,128]{2,1,0:T(8,128)(2,1)}), bf16[8,64,128]{2,1,0:T(8,128)(2,1)S(1)}, u32[]{:S(2)}, u32[]{:S(2)}) %all-to-all-start.2) | async-done | bytes 131104 | tf_op jit(solution)/shard_map/all_to_all | solution.py:75
  86.0 8.2 %all-to-all-start.3 = ((f32[96,2,128]{2,1,0:T(2,128)}), f32[96,2,128]{2,1,0:T(2,128)S(1)}, u32[]{:S(2)}, u32[]{:S(2)}) async-start(f32[96,2,128]{2,1,0:T(2,128)} %bitcast.22), calls=%async_computation.3 | async-start | bytes 196608 | tf_op jit(solution)/shard_map/all_to_all | solution.py:78
  94.5 1.0 fusion.21
  95.6 0.3 copy.14
  95.9 450.9 %all-reduce.2.cloned.1.call-done = f32[128,128]{1,0:T(8,128)} async-done(((f32[128,128]{1,0:T(8,128)}), f32[128,128]{1,0:T(8,128)}) %all-reduce.2.cloned.1.call-update) | async-done | bytes 65552 | tf_op jit(solution)/shard_map/psum | solution.py:56
  546.9 1.5 broadcast_multiply_fusion
  548.3 3.7 scatter_custom_fusion
  552.0 2.0 scatter_fusion
  554.0 0.8 convert_element_type.35
  (31 shorter events, 0.8 us)
Async XLA Ops:
  7.2 1.1 copy-start
  7.2 41.6 %copy-start.6 = (s32[1,2,48]{2,1,0:T(2,128)S(1)}, s32[1,2,48]{2,1,0:T(2,128)}, u32[]{:S(2)}) copy-start(s32[1,2,48]{2,1,0:T(2,128)} %param.15) | copy-start | bytes 1156
  7.2 49.5 %copy-start.4 = (bf16[2048,128]{1,0:T(8,128)(2,1)S(1)}, bf16[2048,128]{1,0:T(8,128)(2,1)}, u32[]{:S(2)}) copy-start(bf16[2048,128]{1,0:T(8,128)(2,1)} %param.9) | copy-start | bytes 1572868
  9.6 32.3 %all-to-all-start.1 = ((bf16[96,2,128]{2,1,0:T(2,128)(2,1)}), bf16[96,2,128]{2,1,0:T(2,128)(2,1)S(1)}, u32[]{:S(2)}, u32[]{:S(2)}) async-start(bf16[96,2,128]{2,1,0:T(2,128)(2,1)} %bitcast.7), calls=%async_computation.1 | async-start | bytes 98304 | tf_op jit(solution)/shard_map/all_to_all | solution.py:30
  41.9 14.8 %all-to-all-start = ((bf16[8,64,128]{2,1,0:T(8,128)(2,1)}), bf16[8,64,128]{2,1,0:T(8,128)(2,1)S(1)}, u32[]{:S(2)}, u32[]{:S(2)}) async-start(bf16[8,64,128]{2,1,0:T(8,128)(2,1)} %bitcast.4), calls=%async_computation | async-start | bytes 262144 | tf_op jit(solution)/shard_map/all_to_all | solution.py:29
  57.1 2.0 copy-start.1
  61.1 3.1 copy-start.5
  61.2 3.1 copy-start.7
  65.8 0.8 copy-start.2
  74.7 11.3 %all-to-all-start.2 = ((bf16[8,64,128]{2,1,0:T(8,128)(2,1)}), bf16[8,64,128]{2,1,0:T(8,128)(2,1)S(1)}, u32[]{:S(2)}, u32[]{:S(2)}) async-start(bf16[8,64,128]{2,1,0:T(8,128)(2,1)} %bitcast.19), calls=%async_computation.2 | async-start | bytes 262144 | tf_op jit(solution)/shard_map/all_to_all | solution.py:75
  78.0 16.4 %copy-start.3 = (bf16[2048,128]{1,0:T(8,128)(2,1)S(1)}, bf16[2048,128]{1,0:T(8,128)(2,1)}, u32[]{:S(2)}) copy-start(bf16[2048,128]{1,0:T(8,128)(2,1)} %copy-done.2) | copy-start | bytes 1572868
  86.0 466.1 %all-to-all-start.3 = ((f32[96,2,128]{2,1,0:T(2,128)}), f32[96,2,128]{2,1,0:T(2,128)S(1)}, u32[]{:S(2)}, u32[]{:S(2)}) async-start(f32[96,2,128]{2,1,0:T(2,128)} %bitcast.22), calls=%async_computation.3 | async-start | bytes 196608 | tf_op jit(solution)/shard_map/all_to_all | solution.py:78
  94.2 452.6 %all-reduce.2.cloned.1.call-start = ((), (), s32[]{:S(2)}) async-start(), calls=%async_computation.4 | async-start | bytes 131072 | tf_op jit(solution)/shard_map/psum | solution.py:56
Sparse Core Ops, SparseCore 0:
  101.0 445.7 all-reduce.1
where the time goes:
time: 564 us; the launch traced here: 562 us
  waiting for transfers between devices  474 us (84%)
  starting transfers between devices  38.7 us (7%)
  between operations  14.9 us (3%)
  matrix products  12.8 us (2%)
  local copies, waits for them, and re-layouts  12.1 us (2%)
  other arithmetic  9.24 us (2%)
    psum x1, waiting for transfers between devices, on_device(): weight_sum = lax.psum(weight_part, ('dom', 'sub'))  451 us
    all_to_all x1, starting transfers between devices, on_device(): lax.all_to_all(dom_rows, 'dom', split_axis=0, concat_axis=0, tiled=True)  20 us
  transfers between devices with their start and end apart: 5, of which 4 were waited for; matrix products, arithmetic and copies ran while one was open for 2% of the time, Pallas kernels for 0%

commit v1 on v0

v1 whole, which is shorter than its diff:
```python
import functools

import jax
import jax.numpy as jnp
from jax import lax
from jax.experimental import pallas as pl
from jax.experimental.pallas import tpu as pltpu
from jax.sharding import PartitionSpec as P

BF = jnp.bfloat16
F32 = jnp.float32
I32 = jnp.int32
MESH = pl.DeviceIdType.MESH


def iota(shape, dim):
    return lax.broadcasted_iota(I32, shape, dim)


def dot(a, b):
    return jnp.dot(a, b, preferred_element_type=F32)


def dot_tn(a, b):
    return lax.dot_general(a, b, (((0,), (0,)), ((), ())), preferred_element_type=F32)


def dot_nt(a, b):
    return lax.dot_general(a, b, (((1,), (1,)), ((), ())), preferred_element_type=F32)


def slot_order(t, rb, nh):
    return jnp.where(t < nh, t + rb, jnp.where(t < nh + rb, t - nh, t))


def kernel(
    c,
    feats, stale, weight, cot, send_sub, send_dom, meta_s, tiles_hbm,
    hidden, wgrad, fgrad,
    st, xcols, tiles, cotv, chain, gbuf, aggv, gzv,
    ohg, ohs, sub_out, g_out, g_in, z_out, back, rsub, rz, rg_out, rg_in, rdom,
    wpart, py, pg_out, pg, pz_out, pz, ag, agy,
    sem_in, ss, rs,
):
    ns, ng, nz, tile, rb, nh, slots = c.ns, c.ng, c.nz, c.tile, c.rb, c.nh, c.slots
    rows, cb, ssub, sdom = c.rows, c.cb, c.ssub, c.sdom
    sub_total, dom_total = ns * ssub, ng * nz * sdom
    gpad = c.gpad
    d = lax.axis_index("dom")
    me_s = lax.axis_index("sub")
    me_z, me_g = d // ng, d % ng

    stale_cp = pltpu.make_async_copy(stale, st, sem_in.at[0])
    feats_cp = pltpu.make_async_copy(feats, xcols.at[pl.ds(0, rb)], sem_in.at[1])
    tiles_cp = pltpu.make_async_copy(tiles_hbm, tiles, sem_in.at[2])
    cot_cp = pltpu.make_async_copy(cot, cotv, sem_in.at[3])
    stale_cp.start()
    feats_cp.start()
    tiles_cp.start()
    cot_cp.start()

    def at_sub(k):
        peer = lax.rem(me_s + k, ns)
        return peer, {"dom": d, "sub": peer}

    def at_g(k):
        peer = lax.rem(me_g + k, ng)
        return peer, {"dom": me_z * ng + peer, "sub": me_s}

    def at_z(k):
        peer = lax.rem(me_z + k, nz)
        return peer, {"dom": peer * ng + me_g, "sub": me_s}

    barrier = pltpu.get_barrier_semaphore()
    for n, where in ((ng, at_g), (nz, at_z), (ns, at_sub)):

        def greet(k, carry, where=where):
            pl.semaphore_signal(barrier, inc=1, device_id=where(k)[1], device_id_type=MESH)
            return carry

        lax.fori_loop(1, n, greet, 0)

    def exchange(phase, n, where, src, dst):
        def copy(k):
            peer, device = where(k)
            return pltpu.make_async_remote_copy(
                src_ref=src(peer),
                dst_ref=dst,
                send_sem=ss.at[phase, k],
                recv_sem=rs.at[phase, k],
                device_id=device,
                device_id_type=MESH,
            )

        def each(act):
            def step(k, carry):
                act(copy(k))
                return carry

            lax.fori_loop(1, n, step, 0)

        return (
            lambda: each(lambda m: m.start()),
            lambda: each(lambda m: m.wait_recv()),
            lambda: each(lambda m: m.wait_send()),
        )

    sub_t = jnp.transpose(jnp.concatenate([send_sub[...], jnp.zeros((ns, 128 - ssub), I32)], axis=1))
    lane_n = iota((1, rows), 1)
    for j in range(ns):
        ohg[j * ssub : (j + 1) * ssub, :] = (sub_t[:ssub, j : j + 1] == lane_n).astype(F32).astype(BF)
    nd = ng * nz
    dom_t = send_dom[...]
    dom_i = jnp.transpose(jnp.concatenate([dom_t, jnp.zeros((sdom, 128 - nd), I32)], axis=1))[:nd]
    for k in range(sdom):
        lo = sub_total + k * nd
        ohg[lo : lo + nd, :] = (dom_i[:, k : k + 1] == lane_n).astype(F32).astype(BF)
    stale_cp.wait()
    picked = dot(ohg[sub_total : sub_total + dom_total, :], st[...]).astype(BF)
    out_r = iota((ng * gpad, dom_total), 0)
    in_r = iota((ng * gpad, dom_total), 1)
    og, ozk = out_r // gpad, out_r % gpad
    want = (ozk % sdom) * nd + (ozk // sdom) * ng + og
    perm = ((want == in_r) & (ozk < nz * sdom)).astype(F32).astype(BF)
    g_out[...] = dot(perm, picked).astype(BF).reshape(g_out.shape)
    pl.semaphore_wait(barrier, ns + ng + nz - 3)
    fg = exchange(0, ng, at_g, lambda p: g_out.at[p], g_in.at[me_g])
    fg[0]()
    g_in[pl.ds(me_g, 1)] = g_out[pl.ds(me_g, 1)]
    sub_out[...] = dot(ohg[0:sub_total, :], st[...]).astype(BF).reshape(sub_out.shape)
    per = tile // ssub
    sub_at = xcols.at[rb + me_s // per, pl.ds(pl.multiple_of(me_s % per * ssub, 16), ssub)]
    fs = exchange(1, ns, at_sub, lambda p: sub_out.at[p], sub_at)
    fs[0]()
    sub_at[...] = sub_out[me_s]
    spare = (sub_total + dom_total) % tile
    if spare:
        xcols[cb - 1, spare:, :] = jnp.zeros((tile - spare, xcols.shape[2]), BF)

    fg[1]()
    out_r = iota((dom_total, ng * gpad), 0)
    in_r = iota((dom_total, ng * gpad), 1)
    oz, ogk = out_r // (ng * sdom), out_r % (ng * sdom)
    want = (ogk // sdom) * gpad + oz * sdom + ogk % sdom
    turn_z = (want == in_r).astype(F32).astype(BF)
    z_out[...] = dot(turn_z, g_in[...].reshape(ng * gpad, -1)).astype(BF).reshape(z_out.shape)
    zrows = ng * sdom
    z_row = sub_total + me_z * zrows
    z_at = xcols.at[rb + z_row // tile, pl.ds(pl.multiple_of(z_row % tile, 16), zrows)]
    fz = exchange(2, nz, at_z, lambda p: z_out.at[p], z_at)
    fz[0]()
    z_at[...] = z_out[me_z]

    feats_cp.wait()
    tiles_cp.wait()
    for p in range(rb):
        chain[p] = dot(tiles[nh + p], xcols[p])
    cot_cp.wait()
    node = iota((rows, 1), 0)
    for j in range(ns):
        ohs[:, j * ssub : (j + 1) * ssub] = (send_sub[j : j + 1, :] == node).astype(F32).astype(BF)
    fs[1]()
    fz[1]()

    for s in (*range(nh), *range(nh + rb, slots)):
        p = s + rb if s < nh else s
        if s < nh:
            block = xcols[rb + s]
        else:
            block = xcols[meta_s[1, s]]
        chain[p] = dot(tiles[s], block) + chain[meta_s[2, s]]

    step = c.step
    w = weight[...]
    for b in range(rb // step):
        lo, hi = b * step * tile, (b + 1) * step * tile
        for r in range(b * step, (b + 1) * step):
            aggv[r * tile : (r + 1) * tile, :] = chain[meta_s[3, r]].astype(BF)
        agg = aggv[lo:hi, :]
        pre = dot(agg, w)
        sig = jax.nn.sigmoid(pre)
        hidden[lo:hi, :] = (pre * sig).astype(BF)
        gz = (cotv[lo:hi, :].astype(F32) * sig * (1.0 + pre * (1.0 - sig))).astype(BF)
        gzv[lo:hi, :] = gz
        gbuf[b * step : (b + 1) * step] = dot_nt(gz, w).astype(BF).reshape(step, tile, -1)
    wpart[...] = dot_tn(aggv[...], gzv[...]).reshape(wpart.shape)
    w1 = exchange(3, ns, at_sub, lambda p: wpart.at[p], py.at[me_s])
    w1[0]()
    py[pl.ds(me_s, 1)] = wpart[pl.ds(me_s, 1)]

    for s in range(slots):
        p = s + rb if s < nh else (s - nh if s < nh + rb else s)
        if nh <= s < nh + rb:
            block = gbuf[s - nh]
        else:
            block = gbuf[meta_s[0, s]]
        term = dot_tn(tiles[s], block)
        chain[p] = term if p < cb else term + chain[meta_s[4, s]]
    for h in range(nh):
        back[h * tile : (h + 1) * tile, :] = chain[meta_s[5, rb + h]].astype(BF)
    bz = exchange(4, nz, at_z, lambda p: back.at[pl.ds(pl.multiple_of(sub_total + p * zrows, 16), zrows)], rz.at[me_z])
    bz[0]()
    rz[pl.ds(me_z, 1)] = back[pl.ds(pl.multiple_of(sub_total + me_z * zrows, 16), zrows), :].reshape(1, zrows, -1)
    bs = exchange(5, ns, at_sub, lambda p: back.at[pl.ds(pl.multiple_of(p * ssub, 16), ssub)], rsub.at[pl.ds(pl.multiple_of(me_s * ssub, 16), ssub)])
    bs[0]()
    rsub[pl.ds(pl.multiple_of(me_s * ssub, 16), ssub), :] = back[pl.ds(pl.multiple_of(me_s * ssub, 16), ssub), :]

    w1[1]()
    part = py[0]
    for i in range(1, ns):
        part = part + py[i]
    rg = part.shape[0] // ng
    for i in range(ng):
        pg_out[i] = part[i * rg : (i + 1) * rg, :]
    w2 = exchange(6, ng, at_g, lambda p: pg_out.at[p], pg.at[me_g])
    w2[0]()
    pg[pl.ds(me_g, 1)] = pg_out[pl.ds(me_g, 1)]

    bz[1]()
    out_r = iota((ng * gpad, dom_total), 0)
    in_r = iota((ng * gpad, dom_total), 1)
    og, ozk = out_r // gpad, out_r % gpad
    want = (ozk // sdom) * zrows + og * sdom + ozk % sdom
    turn_g = ((want == in_r) & (ozk < nz * sdom)).astype(F32).astype(BF)
    rg_out[...] = dot(turn_g, rz[...].reshape(dom_total, -1)).astype(BF).reshape(rg_out.shape)
    bg = exchange(7, ng, at_g, lambda p: rg_out.at[p], rg_in.at[me_g])
    bg[0]()
    rg_in[pl.ds(me_g, 1)] = rg_out[pl.ds(me_g, 1)]

    w2[1]()
    part = pg[0]
    for i in range(1, ng):
        part = part + pg[i]
    pz_out[...] = part
    w3 = exchange(8, nz, at_z, lambda p: pz_out, pz.at[me_z])
    w3[0]()
    pz[pl.ds(me_z, 1)] = part[None]

    bs[1]()
    bg[1]()
    out_r = iota((dom_total, ng * gpad), 0)
    in_r = iota((dom_total, ng * gpad), 1)
    ok, ozg = out_r // nd, out_r % nd
    want = (ozg % ng) * gpad + (ozg // ng) * sdom + ok
    turn_k = (want == in_r).astype(F32).astype(BF)
    rdom[...] = dot(turn_k, rg_in[...].reshape(ng * gpad, -1)).astype(BF)

    w3[1]()
    part = pz[0]
    for i in range(1, nz):
        part = part + pz[i]
    part = part * c.scale
    pz_out2 = pg_out.at[0]
    w2[2]()
    pz_out2[...] = part
    w4 = exchange(9, ng, at_g, lambda p: pz_out2, ag.at[me_g])
    w4[0]()
    ag[pl.ds(me_g, 1)] = part[None]

    def total(b):
        lo, hi = b * step * tile, (b + 1) * step * tile
        acc = dot(ohs[lo:hi, 0:sub_total], rsub[...])
        node_b = lo + iota((hi - lo, 1), 0)
        for k in range(sdom):
            oh = (dom_t[k : k + 1, :] == node_b).astype(F32).astype(BF)
            acc = acc + dot(oh, rdom[k * nd : (k + 1) * nd, :])
        for r in range(step):
            x = chain[meta_s[5, b * step + r]] + acc[r * tile : (r + 1) * tile, :]
            fgrad[lo + r * tile : lo + (r + 1) * tile, :] = x.astype(BF)

    n_b = rb // step
    for b in range(n_b // 2):
        total(b)

    w4[1]()
    w1[2]()
    for i in range(ng):
        wpart[0, i * rg : (i + 1) * rg, :] = ag[i]
    w5 = exchange(10, ns, at_sub, lambda p: wpart.at[0], agy.at[me_s])
    w5[0]()
    agy[pl.ds(me_s, 1)] = wpart[0:1]
    for b in range(n_b // 2, n_b):
        total(b)
    w5[1]()
    wgrad[...] = agy[...].reshape(wgrad.shape)
    for x in (fg, fs, fz, bz, bs, bg, w3, w4, w5):
        x[2]()


def slot_chains(rb, nh, slots, tile_index, tile_count, out):
    out[...] = jnp.zeros_like(out)
    out[0:2, 0:slots] = tile_index[0]
    lanes = out.shape[1]
    count = tile_count[0]
    picks = out[...]
    u = iota((lanes, lanes), 0)
    t = iota((lanes, lanes), 1)
    ord_u = slot_order(u, rb, nh)
    ord_t = slot_order(t, rb, nh)
    for which in range(2):
        line = jnp.broadcast_to(picks[which : which + 1, :], (lanes, lanes))
        turned = line.T
        prev = jnp.where((turned == line) & (ord_u < ord_t) & (u < slots), ord_u, 0)
        last = jnp.where((turned == t) & (u < count), ord_u, 0)
        out[2 + 2 * which : 3 + 2 * which, :] = jnp.max(prev, axis=0, keepdims=True)
        out[3 + 2 * which : 4 + 2 * which, :] = jnp.max(last, axis=0, keepdims=True)


class Sizes:
    pass


def on_device(feats, stale, weight, cot, send_sub, send_dom, tile_index, tile_count, tiles):
    c = Sizes()
    c.rows, f = feats.shape
    c.slots, c.tile = tiles.shape[0], tiles.shape[1]
    c.rb = c.rows // c.tile
    c.ns, c.ssub = send_sub.shape
    nd, c.sdom = send_dom.shape
    c.ng = 16 // c.sdom
    c.nz = nd // c.ng
    halo = c.ns * c.ssub + nd * c.sdom
    c.nh = -(-halo // c.tile)
    c.cb = c.rb + c.nh
    c.gpad = -(-c.nz * c.sdom // 16) * 16
    c.step = max(1, c.rb // 4)
    c.scale = float(1.0 / (c.rows * nd * c.ns) ** 0.5)
    hid = weight.shape[1]
    sub_total, dom_total = c.ns * c.ssub, nd * c.sdom
    ry = f // c.ns
    rg = ry // c.ng
    vmem = pl.BlockSpec(memory_space=pltpu.VMEM)
    smem = pl.BlockSpec(memory_space=pltpu.SMEM)
    hbm = pl.BlockSpec(memory_space=pltpu.HBM)
    meta = pl.pallas_call(
        functools.partial(slot_chains, c.rb, c.nh, c.slots),
        out_shape=jax.ShapeDtypeStruct((8, 128), I32),
        in_specs=[vmem, smem],
        out_specs=vmem,
    )(tile_index, tile_count)
    scratch = [
        pltpu.VMEM((c.rows, f), BF),
        pltpu.VMEM((c.cb, c.tile, f), BF),
        pltpu.VMEM((c.slots, c.tile, c.tile), BF),
        pltpu.VMEM((c.rows, hid), BF),
        pltpu.VMEM((c.slots, c.tile, f), F32),
        pltpu.VMEM((c.rb, c.tile, f), BF),
        pltpu.VMEM((c.rows, f), BF),
        pltpu.VMEM((c.rows, hid), BF),
        pltpu.VMEM((sub_total + dom_total, c.rows), BF),
        pltpu.VMEM((c.rows, sub_total), BF),
        pltpu.VMEM((c.ns, c.ssub, f), BF),
        pltpu.VMEM((c.ng, c.gpad, f), BF),
        pltpu.VMEM((c.ng, c.gpad, f), BF),
        pltpu.VMEM((c.nz, c.ng * c.sdom, f), BF),
        pltpu.VMEM((c.nh * c.tile, f), BF),
        pltpu.VMEM((sub_total, f), BF),
        pltpu.VMEM((c.nz, c.ng * c.sdom, f), BF),
        pltpu.VMEM((c.ng, c.gpad, f), BF),
        pltpu.VMEM((c.ng, c.gpad, f), BF),
        pltpu.VMEM((dom_total, f), BF),
        pltpu.VMEM((c.ns, ry, hid), F32),
        pltpu.VMEM((c.ns, ry, hid), F32),
        pltpu.VMEM((c.ng, rg, hid), F32),
        pltpu.VMEM((c.ng, rg, hid), F32),
        pltpu.VMEM((rg, hid), F32),
        pltpu.VMEM((c.nz, rg, hid), F32),
        pltpu.VMEM((c.ng, rg, hid), F32),
        pltpu.VMEM((c.ns, ry, hid), F32),
        pltpu.SemaphoreType.DMA((4,)),
        pltpu.SemaphoreType.DMA((11, max(c.ns, c.ng, c.nz))),
        pltpu.SemaphoreType.DMA((11, max(c.ns, c.ng, c.nz))),
    ]
    return pl.pallas_call(
        functools.partial(kernel, c),
        out_shape=(
            jax.ShapeDtypeStruct((c.rows, hid), BF),
            jax.ShapeDtypeStruct((f, hid), F32),
            jax.ShapeDtypeStruct((c.rows, f), BF),
        ),
        in_specs=[hbm, hbm, vmem, hbm, vmem, vmem, smem, hbm],
        out_specs=(vmem, vmem, vmem),
        scratch_shapes=scratch,
        compiler_params=pltpu.CompilerParams(
            collective_id=0, has_side_effects=True, vmem_limit_bytes=48 * 1024 * 1024
        ),
    )(feats.reshape(c.rb, c.tile, f), stale, weight, cot, send_sub, send_dom.T, meta, tiles)


def solution(mesh):
    rows = P(("dom", "sub"), None)
    cube = P(("dom", "sub"), None, None)
    return jax.shard_map(
        on_device,
        mesh=mesh,
        in_specs=(rows, rows, P(), rows, rows, rows, cube, P(("dom", "sub")), cube),
        out_specs=(rows, P(), rows),
        check_vma=False,
    )
```

time: 564 us -> 70.8 us (0.13)
  waiting for transfers between devices: 474 us -> 0 us
  Pallas kernels: 0 us -> 59.4 us
  starting transfers between devices: 38.7 us -> 0 us
  between operations: 14.9 us -> 1.29 us
  matrix products: 12.8 us -> 0 us
  other arithmetic: 9.24 us -> 0 us
    psum x1 -> x0, waiting for transfers between devices: 451 us -> none  [on_device(): weight_sum = lax.psum(weight_part, ('dom', 'sub'))]
    pallas_call x0 -> x2, Pallas kernels: none -> 59.4 us  [the longest x1 58.1 us: on_device(): pl.pallas_call(functools.partial(kernel, c), out_shape=(jax.ShapeDtypeStr...]
    all_to_all x4 -> x0, starting transfers between devices: 38.4 us -> none  [the longest x1 20 us: on_device(): lax.all_to_all(dom_rows, 'dom', split_axis=0, concat_axis=0, tiled=True)]
    all_to_all x4 -> x0, waiting for transfers between devices: 23 us -> none  [the longest x1 8.1 us: on_device(): lax.all_to_all(dom_rows, 'dom', split_axis=0, concat_axis=0, tiled=True)]
    dot_general x7 -> x0, matrix products: 12.8 us -> none  [the longest x1 2.95 us: on_device(): jnp.einsum('ct,tif->cif', col_onehot, back_terms, precision=lax.Precision...]
    unnamed x17 -> x19, local copies, waits for them, and re-layouts: 1.7 us -> 9.56 us
    gather x4 -> x0, local copies, waits for them, and re-layouts: 7.25 us -> none  [the longest x1 1.97 us: on_device(): grad_blocks = grad_agg.reshape(row_blocks, tile_size, feat_width)[row_pick]]
    scatter-add x2 -> x0, other arithmetic: 5.69 us -> none  [the longest x1 3.7 us: on_device(): own_grad.at[send_sub.reshape(-1)].add(return_sub.reshape(-1, feat_width))]
  transfers between devices with their start and end apart: 5 -> 0, of which waited for: 4 -> 0; matrix products, arithmetic and copies ran while one was open for 2% -> 0% of each run, Pallas kernels for 0% -> 0%
where the time goes in v1:
time: 70.8 us; the launch traced here: 70.3 us
  Pallas kernels  59.4 us (84%)
  local copies, waits for them, and re-layouts  9.56 us (14%)
  between operations  1.29 us (2%)
    pallas_call x1, Pallas kernels, on_device(): pl.pallas_call(functools.partial(kernel, c), out_shape=(jax.ShapeDtypeStr...  58.1 us
    unnamed x19, local copies, waits for them, and re-layouts  9.56 us

profile of v1, /device:TPU:1, one launch (start us, length us, event | category | flops | bytes accessed | tf_op | source)
XLA Modules:
  0.0 70.3 jit_solution(3442789258618310993)
XLA Ops:
  1.3 1.4 %shard_map.112.meta_s = s32[8,128]{1,0:T(8,128)} custom-call(s32[1,2,48]{2,1,0:T(2,128)} %tile_index.1, s32[1]{0:T(128)S(6)} %copy.15.tile_count), custom_call_target="tpu_custom_call" | custom-call | tf_op jit(solution)/shard_map/pallas_call | solution.py:335
  2.7 0.0 copy-start
  2.7 1.4 %copy-done = bf16[48,128,128]{2,1,0:T(8,128)(2,1)S(1)} copy-done((bf16[48,128,128]{2,1,0:T(8,128)(2,1)S(1)}, bf16[48,128,128]{2,1,0:T(8,128)(2,1)}, u32[]{:S(2)}) %copy-start) | copy-done | bytes 1572888
  4.1 0.0 copy-start.1
  4.1 1.0 %copy-done.1 = bf16[2048,128]{1,0:T(8,128)(2,1)S(1)} copy-done((bf16[2048,128]{1,0:T(8,128)(2,1)S(1)}, bf16[2048,128]{1,0:T(8,128)(2,1)}, u32[]{:S(2)}) %copy-start.1) | copy-done | bytes 524312
  5.1 0.0 copy-start.2
  5.1 1.0 %copy-done.2 = bf16[2048,128]{1,0:T(8,128)(2,1)S(1)} copy-done((bf16[2048,128]{1,0:T(8,128)(2,1)S(1)}, bf16[2048,128]{1,0:T(8,128)(2,1)}, u32[]{:S(2)}) %copy-start.2) | copy-done | bytes 524312
  6.2 0.0 copy-start.3
  6.2 1.0 %copy-done.3 = bf16[2048,128]{1,0:T(8,128)(2,1)S(1)} copy-done((bf16[2048,128]{1,0:T(8,128)(2,1)S(1)}, bf16[2048,128]{1,0:T(8,128)(2,1)}, u32[]{:S(2)}) %copy-start.3) | copy-done | bytes 524312
  7.2 0.0 copy-start.4
  7.2 0.8 %copy-done.4 = bf16[128,128]{1,0:T(8,128)(2,1)S(1)} copy-done((bf16[128,128]{1,0:T(8,128)(2,1)S(1)}, bf16[128,128]{1,0:T(8,128)(2,1)}, u32[]{:S(2)}) %copy-start.4) | copy-done | bytes 32792
  8.0 0.0 copy-start.5
  8.0 0.7 copy-done.5
  8.6 0.0 copy-start.6
  8.6 0.7 copy-done.6
  9.3 0.0 copy-start.7
  9.3 0.7 copy-done.7
  10.0 58.1 %shard_map.113 = (bf16[2048,128]{1,0:T(8,128)(2,1)S(1)}, f32[128,128]{1,0:T(8,128)S(1)}, bf16[2048,128]{1,0:T(8,128)(2,1)S(1)}) custom-call(bf16[16,128,128]{2,1,0:T(8,128)(2,1)S(1)} %bitcast.2, bf16[2048,128]{1,0:T(8,128)(2,1)S(1)} %copy-done.2, bf16[128,128]{1,0:T(8,128)(2,1)S(1)} %copy-done.4, bf16[2048,128]{1,0:T(8,128)(2,1)S(1)} %copy-done.3, ...), custom_call_target="tpu_custom_call" | custom-call | tf_op jit(solution)/shard_map/pallas_call | solution.py:374
  68.1 0.8 %copy.16 = bf16[2048,128]{1,0:T(8,128)(2,1)} copy(bf16[2048,128]{1,0:T(8,128)(2,1)S(1)} %get-tuple-element.6) | data formatting | bytes 1048576
  68.9 0.6 copy.17
  69.5 0.8 %copy.18 = bf16[2048,128]{1,0:T(8,128)(2,1)} copy(bf16[2048,128]{1,0:T(8,128)(2,1)S(1)} %get-tuple-element.8) | data formatting | bytes 1048576
Async XLA Ops:
  2.7 1.4 %copy-start = (bf16[48,128,128]{2,1,0:T(8,128)(2,1)S(1)}, bf16[48,128,128]{2,1,0:T(8,128)(2,1)}, u32[]{:S(2)}) copy-start(bf16[48,128,128]{2,1,0:T(8,128)(2,1)} %tiles_hbm.1) | copy-start | bytes 4718596
  4.1 1.0 %copy-start.1 = (bf16[2048,128]{1,0:T(8,128)(2,1)S(1)}, bf16[2048,128]{1,0:T(8,128)(2,1)}, u32[]{:S(2)}) copy-start(bf16[2048,128]{1,0:T(8,128)(2,1)} %param.9) | copy-start | bytes 1572868
  5.1 1.0 %copy-start.2 = (bf16[2048,128]{1,0:T(8,128)(2,1)S(1)}, bf16[2048,128]{1,0:T(8,128)(2,1)}, u32[]{:S(2)}) copy-start(bf16[2048,128]{1,0:T(8,128)(2,1)} %stale.1) | copy-start | bytes 1572868
  6.2 1.0 %copy-start.3 = (bf16[2048,128]{1,0:T(8,128)(2,1)S(1)}, bf16[2048,128]{1,0:T(8,128)(2,1)}, u32[]{:S(2)}) copy-start(bf16[2048,128]{1,0:T(8,128)(2,1)} %cot.1) | copy-start | bytes 1572868
  7.2 0.8 %copy-start.4 = (bf16[128,128]{1,0:T(8,128)(2,1)S(1)}, bf16[128,128]{1,0:T(8,128)(2,1)}, u32[]{:S(2)}) copy-start(bf16[128,128]{1,0:T(8,128)(2,1)} %weight.1) | copy-start | bytes 98308
  8.0 0.7 copy-start.5
  8.6 0.7 copy-start.6
  9.3 0.7 copy-start.7

commit v2 on v1

v2 whole, which is shorter than its diff:
```python
import functools

import jax
import jax.numpy as jnp
from jax import lax
from jax.experimental import pallas as pl
from jax.experimental.pallas import tpu as pltpu
from jax.sharding import PartitionSpec as P

BF = jnp.bfloat16
F32 = jnp.float32
I32 = jnp.int32
MESH = pl.DeviceIdType.MESH


def iota(shape, dim):
    return lax.broadcasted_iota(I32, shape, dim)


def dot(a, b):
    return jnp.dot(a, b, preferred_element_type=F32)


def dot_tn(a, b):
    return lax.dot_general(a, b, (((0,), (0,)), ((), ())), preferred_element_type=F32)


def dot_nt(a, b):
    return lax.dot_general(a, b, (((1,), (1,)), ((), ())), preferred_element_type=F32)


def one_hot(hit):
    return hit.astype(F32).astype(BF)


def slot_order(t, rb, nh):
    return jnp.where(t < nh, t + rb, jnp.where(t < nh + rb, t - nh, t))


def wrap(i, n):
    return jnp.where(i >= n, i - n, i)


class Exchange:
    def __init__(self, group, src, dst, block, ss, rs):
        self.copies = [
            pltpu.make_async_remote_copy(
                src_ref=src(peer), dst_ref=dst, send_sem=ss, recv_sem=rs, device_id=device, device_id_type=MESH
            )
            for peer, device in group
        ]
        self.block, self.ss, self.rs = block, ss, rs

    def start(self):
        for copy in self.copies:
            copy.start()

    def arrived(self):
        pltpu.make_async_copy(self.block, self.block, self.rs).wait()

    def left(self):
        pltpu.make_async_copy(self.block, self.block, self.ss).wait()


def kernel(
    c,
    feats, stale, weight, cot, send_sub, send_dom, meta_s, tiles_hbm,
    hidden_hbm, wgrad_hbm, fgrad_hbm,
    st, xcols, tiles, cotv, chain, gbuf, aggv, gzv,
    ohg, ohs, ohd, sub_out, g_out, g_in, z_out, back, rsub, rz, rg_out, rg_in, rdom,
    wp_out, wp_in, wm_out, wm_in, wa_out, wa_in, hidden, fgrad, wgrad, acc,
    sem_in, ss, rs,
):
    ns, ng, nz, tile, rb, nh, slots = c.ns, c.ng, c.nz, c.tile, c.rb, c.nh, c.slots
    rows, cb, ssub, sdom = c.rows, c.cb, c.ssub, c.sdom
    sub_total, dom_total = ns * ssub, ng * nz * sdom
    nd = ng * nz
    gpad, nl = c.gpad, c.nl
    d = lax.axis_index("dom")
    me_s = lax.axis_index("sub")
    me_z, me_g = d // ng, d % ng
    me_h, me_l = me_g // nl, me_g % nl

    stale_cp = pltpu.make_async_copy(stale, st, sem_in.at[0])
    feats_cp = pltpu.make_async_copy(feats, xcols.at[pl.ds(0, rb)], sem_in.at[1])
    tiles_cp = pltpu.make_async_copy(tiles_hbm, tiles, sem_in.at[2])
    cot_cp = pltpu.make_async_copy(cot, cotv, sem_in.at[3])
    hidden_cp = pltpu.make_async_copy(hidden, hidden_hbm, sem_in.at[4])
    fgrad_cp = pltpu.make_async_copy(fgrad, fgrad_hbm, sem_in.at[5])
    wgrad_cp = pltpu.make_async_copy(wgrad, wgrad_hbm, sem_in.at[6])
    stale_cp.start()
    feats_cp.start()
    tiles_cp.start()
    cot_cp.start()

    def along(*steps):
        sizes = (ns, nl, ng // nl, nz)
        mine = (me_s, me_l, me_h, me_z)
        offsets = [()]
        for axis in range(4):
            offsets = [o + (k,) for o in offsets for k in range(sizes[axis] if axis in steps else 1)]
        group = []
        for offset in offsets[1:]:
            at = [wrap(m + o, n) if o else m for m, o, n in zip(mine, offset, sizes)]
            index = 0
            for axis in reversed(range(4)):
                if axis in steps:
                    index = index * sizes[axis] + at[axis]
            s, l, h, z = at
            group.append((index, {"dom": (z * (ng // nl) + h) * nl + l, "sub": s}))
        return group

    by_sub, by_g, by_z = along(0), along(1, 2), along(3)
    by_piece, by_rest = along(0, 1), along(2, 3)
    barrier = pltpu.get_barrier_semaphore()
    for _, device in (*by_g, *by_z, *by_sub):
        pl.semaphore_signal(barrier, inc=1, device_id=device, device_id_type=MESH)

    lane_n = iota((1, rows), 1)
    dom_t = send_dom[...]
    dom_i = jnp.transpose(jnp.concatenate([dom_t, jnp.zeros((sdom, 128 - nd), I32)], axis=1))[:nd]
    for k in range(sdom):
        ohg[sub_total + k * nd : sub_total + (k + 1) * nd, :] = one_hot(dom_i[:, k : k + 1] == lane_n)
    stale_cp.wait()
    picked = dot(ohg[sub_total:, :], st[...]).astype(BF)
    out_r = iota((ng * gpad, dom_total), 0)
    in_r = iota((ng * gpad, dom_total), 1)
    og, ozk = out_r // gpad, out_r % gpad
    want = (ozk % sdom) * nd + (ozk // sdom) * ng + og
    perm = one_hot((want == in_r) & (ozk < nz * sdom))
    g_out[...] = dot(perm, picked).astype(BF).reshape(g_out.shape)
    pl.semaphore_wait(barrier, ns + ng + nz - 3)
    fg = Exchange(by_g, lambda p: g_out.at[p], g_in.at[me_g], g_in.at[pl.ds(0, ng - 1)], ss.at[0], rs.at[0])
    fg.start()
    g_in[pl.ds(me_g, 1)] = g_out[pl.ds(me_g, 1)]

    sub_t = jnp.transpose(jnp.concatenate([send_sub[...], jnp.zeros((ns, 128 - ssub), I32)], axis=1))
    for j in range(ns):
        ohg[j * ssub : (j + 1) * ssub, :] = one_hot(sub_t[:ssub, j : j + 1] == lane_n)
    sub_out[...] = dot(ohg[0:sub_total, :], st[...]).astype(BF).reshape(sub_out.shape)
    per = tile // ssub
    sub_at = xcols.at[rb + me_s // per, pl.ds(pl.multiple_of(me_s % per * ssub, 16), ssub)]
    fs = Exchange(by_sub, lambda p: sub_out.at[p], sub_at, sub_out.at[pl.ds(0, ns - 1)], ss.at[1], rs.at[1])
    fs.start()
    sub_at[...] = sub_out[me_s]
    spare = (sub_total + dom_total) % tile
    if spare:
        xcols[cb - 1, spare:, :] = jnp.zeros((tile - spare, xcols.shape[2]), BF)

    out_r = iota((dom_total, ng * gpad), 0)
    in_r = iota((dom_total, ng * gpad), 1)
    oz, ogk = out_r // (ng * sdom), out_r % (ng * sdom)
    want = (ogk // sdom) * gpad + oz * sdom + ogk % sdom
    turn_z = one_hot(want == in_r)
    fg.arrived()
    z_out[...] = dot(turn_z, g_in[...].reshape(ng * gpad, -1)).astype(BF).reshape(z_out.shape)
    zrows = ng * sdom
    z_row = sub_total + me_z * zrows
    z_at = xcols.at[rb + z_row // tile, pl.ds(pl.multiple_of(z_row % tile, 16), zrows)]
    fz = Exchange(by_z, lambda p: z_out.at[p], z_at, z_out.at[pl.ds(0, nz - 1)], ss.at[2], rs.at[2])
    fz.start()
    z_at[...] = z_out[me_z]

    feats_cp.wait()
    tiles_cp.wait()
    for p in range(rb):
        chain[p] = dot(tiles[nh + p], xcols[p])
    cot_cp.wait()
    node = iota((rows, 1), 0)
    for j in range(sub_total // 128):
        pieces = [send_sub[i : i + 1, :] for i in range(j * 128 // ssub, (j + 1) * 128 // ssub)]
        ohs[:, j * 128 : (j + 1) * 128] = one_hot(jnp.concatenate(pieces, axis=1) == node)
    ohd[...] = one_hot(jnp.concatenate([dom_t[k : k + 1, :] for k in range(sdom)], axis=1) == node)
    fs.arrived()
    fz.arrived()

    for s in (*range(nh), *range(nh + rb, slots)):
        p = s + rb if s < nh else s
        block = xcols[rb + s] if s < nh else xcols[meta_s[1, s]]
        chain[p] = dot(tiles[s], block) + chain[meta_s[2, s]]

    step = c.step
    w = weight[...]
    part = None
    for b in range(rb // step):
        lo, hi = b * step * tile, (b + 1) * step * tile
        for r in range(b * step, (b + 1) * step):
            aggv[r * tile : (r + 1) * tile, :] = chain[meta_s[3, r]].astype(BF)
        agg = aggv[lo:hi, :]
        pre = dot(agg, w)
        sig = jax.nn.sigmoid(pre)
        hidden[lo:hi, :] = (pre * sig).astype(BF)
        gz = (cotv[lo:hi, :].astype(F32) * sig * (1.0 + pre * (1.0 - sig))).astype(BF)
        gzv[lo:hi, :] = gz
        gbuf[b * step : (b + 1) * step] = dot_nt(gz, w).astype(BF).reshape(step, tile, -1)
    part = dot_tn(aggv[...], gzv[...])
    pieces = wp_out.shape[0]
    rp = wp_out.shape[1]
    for i in range(pieces):
        wp_out[i] = part[i * rp : (i + 1) * rp, :]

    me_p = me_l * ns + me_s
    w1 = Exchange(by_piece, lambda p: wp_out.at[p], wp_in.at[me_p], wp_in.at[pl.ds(0, pieces - 1)], ss.at[3], rs.at[3])
    w1.start()
    hidden_cp.start()
    wp_in[pl.ds(me_p, 1)] = wp_out[pl.ds(me_p, 1)]

    for s in range(slots):
        p = s + rb if s < nh else (s - nh if s < nh + rb else s)
        block = gbuf[s - nh] if nh <= s < nh + rb else gbuf[meta_s[0, s]]
        term = dot_tn(tiles[s], block)
        chain[p] = term if p < cb else term + chain[meta_s[4, s]]
    for h in range(nh):
        back[h * tile : (h + 1) * tile, :] = chain[meta_s[5, rb + h]].astype(BF)

    def back_z(p):
        return back.at[pl.ds(pl.multiple_of(sub_total + p * zrows, 16), zrows)]

    def back_s(p):
        return back.at[pl.ds(pl.multiple_of(p * ssub, 16), ssub)]

    bz = Exchange(by_z, back_z, rz.at[me_z], rz.at[pl.ds(0, nz - 1)], ss.at[4], rs.at[4])
    bz.start()
    bs = Exchange(by_sub, back_s, rsub.at[me_s], rsub.at[pl.ds(0, ns - 1)], ss.at[5], rs.at[5])
    bs.start()
    rz[pl.ds(me_z, 1)] = back_z(me_z)[...].reshape(1, zrows, -1)
    rsub[pl.ds(me_s, 1)] = back_s(me_s)[...].reshape(1, ssub, -1)
    out_r = iota((ng * gpad, dom_total), 0)
    in_r = iota((ng * gpad, dom_total), 1)
    og, ozk = out_r // gpad, out_r % gpad
    want = (ozk // sdom) * zrows + og * sdom + ozk % sdom
    turn_g = one_hot((want == in_r) & (ozk < nz * sdom))

    w1.arrived()
    piece = wp_in[0]
    for i in range(1, pieces):
        piece = piece + wp_in[i]
    wm_out[...] = piece
    rest = wm_in.shape[0]
    me_r = me_z * (ng // nl) + me_h
    w2 = Exchange(by_rest, lambda p: wm_out, wm_in.at[me_r], wm_in.at[pl.ds(0, rest - 1)], ss.at[6], rs.at[6])
    w2.start()
    wm_in[pl.ds(me_r, 1)] = piece[None]

    bz.arrived()
    rg_out[...] = dot(turn_g, rz[...].reshape(dom_total, -1)).astype(BF).reshape(rg_out.shape)
    bg = Exchange(by_g, lambda p: rg_out.at[p], rg_in.at[me_g], rg_in.at[pl.ds(0, ng - 1)], ss.at[7], rs.at[7])
    bg.start()
    rg_in[pl.ds(me_g, 1)] = rg_out[pl.ds(me_g, 1)]

    bs.arrived()
    for b in range(rb // step):
        lo, hi = b * step * tile, (b + 1) * step * tile
        got = dot(ohs[lo:hi, :], rsub[...].reshape(sub_total, -1))
        for r in range(step):
            acc[lo + r * tile : lo + (r + 1) * tile, :] = chain[meta_s[5, b * step + r]] + got[r * tile : (r + 1) * tile, :]

    out_r = iota((dom_total, ng * gpad), 0)
    in_r = iota((dom_total, ng * gpad), 1)
    ok, ozg = out_r // nd, out_r % nd
    want = (ozg % ng) * gpad + (ozg // ng) * sdom + ok
    turn_k = one_hot(want == in_r)
    bg.arrived()
    rdom[...] = dot(turn_k, rg_in[...].reshape(ng * gpad, -1)).astype(BF)
    for b in range(rb // step):
        lo, hi = b * step * tile, (b + 1) * step * tile
        fgrad[lo:hi, :] = (acc[lo:hi, :] + dot(ohd[lo:hi, :], rdom[...])).astype(BF)
    fgrad_cp.start()

    w2.arrived()
    piece = wm_in[0]
    for i in range(1, rest):
        piece = piece + wm_in[i]
    piece = piece * c.scale
    wa_out[...] = piece
    w3 = Exchange(by_piece, lambda p: wa_out, wa_in.at[me_p], wa_in.at[pl.ds(0, pieces - 1)], ss.at[8], rs.at[8])
    w3.start()
    wa_in[pl.ds(me_p, 1)] = piece[None]
    for x in (fg, fs, fz, bz, bs, bg, w1, w2):
        x.left()
    hidden_cp.wait()
    fgrad_cp.wait()
    w3.arrived()
    for i in range(pieces):
        wgrad[i * rp : (i + 1) * rp, :] = wa_in[i]
    wgrad_cp.start()
    w3.left()
    wgrad_cp.wait()


def hand_over(*refs):
    for src, dst in zip(refs[:3], refs[3:]):
        dst[...] = src[...]


def slot_chains(rb, nh, slots, tile_index, tile_count, out):
    out[...] = jnp.zeros_like(out)
    out[0:2, 0:slots] = tile_index[0]
    lanes = out.shape[1]
    count = tile_count[0]
    picks = out[...]
    u = iota((lanes, lanes), 0)
    t = iota((lanes, lanes), 1)
    ord_u = slot_order(u, rb, nh)
    ord_t = slot_order(t, rb, nh)
    for which in range(2):
        line = jnp.broadcast_to(picks[which : which + 1, :], (lanes, lanes))
        turned = line.T
        prev = jnp.where((turned == line) & (ord_u < ord_t) & (u < slots), ord_u, 0)
        last = jnp.where((turned == t) & (u < count), ord_u, 0)
        out[2 + 2 * which : 3 + 2 * which, :] = jnp.max(prev, axis=0, keepdims=True)
        out[3 + 2 * which : 4 + 2 * which, :] = jnp.max(last, axis=0, keepdims=True)


class Sizes:
    pass


def on_device(feats, stale, weight, cot, send_sub, send_dom, tile_index, tile_count, tiles):
    c = Sizes()
    c.rows, f = feats.shape
    c.slots, c.tile = tiles.shape[0], tiles.shape[1]
    c.rb = c.rows // c.tile
    c.ns, c.ssub = send_sub.shape
    nd, c.sdom = send_dom.shape
    c.ng = 16 // c.sdom
    c.nz = nd // c.ng
    halo = c.ns * c.ssub + nd * c.sdom
    c.nh = -(-halo // c.tile)
    c.cb = c.rb + c.nh
    c.gpad = -(-c.nz * c.sdom // 16) * 16
    c.step = max(1, c.rb // 4)
    c.scale = float(1.0 / (c.rows * nd * c.ns) ** 0.5)
    hid = weight.shape[1]
    sub_total, dom_total = c.ns * c.ssub, nd * c.sdom
    c.nl = max(1, c.ng // 2)
    pieces, rest = c.ns * c.nl, c.ng // c.nl * c.nz
    rp = f // pieces
    vmem = pl.BlockSpec(memory_space=pltpu.VMEM)
    smem = pl.BlockSpec(memory_space=pltpu.SMEM)
    hbm = pl.BlockSpec(memory_space=pltpu.HBM)
    meta = pl.pallas_call(
        functools.partial(slot_chains, c.rb, c.nh, c.slots),
        out_shape=jax.ShapeDtypeStruct((8, 128), I32),
        in_specs=[vmem, smem],
        out_specs=vmem,
    )(tile_index, tile_count)
    scratch = [
        pltpu.VMEM((c.rows, f), BF),
        pltpu.VMEM((c.cb, c.tile, f), BF),
        pltpu.VMEM((c.slots, c.tile, c.tile), BF),
        pltpu.VMEM((c.rows, hid), BF),
        pltpu.VMEM((c.slots, c.tile, f), F32),
        pltpu.VMEM((c.rb, c.tile, f), BF),
        pltpu.VMEM((c.rows, f), BF),
        pltpu.VMEM((c.rows, hid), BF),
        pltpu.VMEM((sub_total + dom_total, c.rows), BF),
        pltpu.VMEM((c.rows, sub_total), BF),
        pltpu.VMEM((c.rows, dom_total), BF),
        pltpu.VMEM((c.ns, c.ssub, f), BF),
        pltpu.VMEM((c.ng, c.gpad, f), BF),
        pltpu.VMEM((c.ng, c.gpad, f), BF),
        pltpu.VMEM((c.nz, c.ng * c.sdom, f), BF),
        pltpu.VMEM((c.nh * c.tile, f), BF),
        pltpu.VMEM((c.ns, c.ssub, f), BF),
        pltpu.VMEM((c.nz, c.ng * c.sdom, f), BF),
        pltpu.VMEM((c.ng, c.gpad, f), BF),
        pltpu.VMEM((c.ng, c.gpad, f), BF),
        pltpu.VMEM((dom_total, f), BF),
        pltpu.VMEM((pieces, rp, hid), F32),
        pltpu.VMEM((pieces, rp, hid), F32),
        pltpu.VMEM((rp, hid), F32),
        pltpu.VMEM((rest, rp, hid), F32),
        pltpu.VMEM((rp, hid), F32),
        pltpu.VMEM((pieces, rp, hid), F32),
        pltpu.VMEM((c.rows, hid), BF),
        pltpu.VMEM((c.rows, f), BF),
        pltpu.VMEM((f, hid), F32),
        pltpu.VMEM((c.rows, f), F32),
        pltpu.SemaphoreType.DMA((7,)),
        pltpu.SemaphoreType.DMA((9,)),
        pltpu.SemaphoreType.DMA((9,)),
    ]
    outs = (
        jax.ShapeDtypeStruct((c.rows, hid), BF),
        jax.ShapeDtypeStruct((f, hid), F32),
        jax.ShapeDtypeStruct((c.rows, f), BF),
    )
    results = pl.pallas_call(
        functools.partial(kernel, c),
        out_shape=outs,
        in_specs=[hbm, hbm, vmem, hbm, vmem, vmem, smem, hbm],
        out_specs=(hbm, hbm, hbm),
        scratch_shapes=scratch,
        compiler_params=pltpu.CompilerParams(
            collective_id=0, has_side_effects=True, vmem_limit_bytes=63 * 1024 * 1024
        ),
    )(feats.reshape(c.rb, c.tile, f), stale, weight, cot, send_sub, send_dom.T, meta, tiles)
    steps = 4
    blocks = [pl.BlockSpec((o.shape[0] // steps, o.shape[1]), lambda i: (i, 0)) for o in outs]
    return pl.pallas_call(
        hand_over,
        out_shape=outs,
        grid=(steps,),
        in_specs=blocks,
        out_specs=blocks,
    )(*results)


def solution(mesh):
    rows = P(("dom", "sub"), None)
    cube = P(("dom", "sub"), None, None)
    return jax.shard_map(
        on_device,
        mesh=mesh,
        in_specs=(rows, rows, P(), rows, rows, rows, cube, P(("dom", "sub")), cube),
        out_specs=(rows, P(), rows),
        check_vma=False,
    )
```

time: 70.8 us -> 57.2 us (0.81)
  local copies, waits for them, and re-layouts: 9.56 us -> 0 us
  Pallas kernels: 59.4 us -> 55.6 us
    unnamed x19 -> x0, local copies, waits for them, and re-layouts: 9.56 us -> none
    pallas_call x1 -> x2, Pallas kernels: 58.1 us -> 54.2 us  [the longest x1 50.7 us: on_device(): pl.pallas_call(functools.partial(kernel, c), out_shape=outs, in_specs=[hb...]
where the time goes in v2:
time: 57.2 us; the launch traced here: 56.9 us
  Pallas kernels  55.6 us (97%)
  between operations  1.29 us (2%)
    pallas_call x1, Pallas kernels, on_device(): pl.pallas_call(functools.partial(kernel, c), out_shape=outs, in_specs=[hb...  50.7 us
    pallas_call x1, Pallas kernels, on_device(): pl.pallas_call(hand_over, out_shape=outs, grid=(steps,), in_specs=blocks,...  3.46 us
    pallas_call x1, Pallas kernels, on_device(): pl.pallas_call(functools.partial(slot_chains, c.rb, c.nh, c.slots), out_s...  1.39 us

profile of v2, /device:TPU:1, one launch (start us, length us, event | category | flops | bytes accessed | tf_op | source)
XLA Modules:
  0.0 56.9 jit_solution(13271800581778165176)
XLA Ops:
  1.3 1.4 %shard_map.112.meta_s = s32[8,128]{1,0:T(8,128)} custom-call(s32[1,2,48]{2,1,0:T(2,128)} %tile_index.1, s32[1]{0:T(128)S(6)} %copy.12.tile_count), custom_call_target="tpu_custom_call" | custom-call | tf_op jit(solution)/shard_map/pallas_call | solution.py:342
  2.7 50.7 %shard_map.113 = (bf16[2048,128]{1,0:T(8,128)(2,1)}, f32[128,128]{1,0:T(8,128)}, bf16[2048,128]{1,0:T(8,128)(2,1)}) custom-call(bf16[16,128,128]{2,1,0:T(8,128)(2,1)} %bitcast.2, bf16[2048,128]{1,0:T(8,128)(2,1)} %stale.1, bf16[128,128]{1,0:T(8,128)(2,1)} %weight.1, bf16[2048,128]{1,0:T(8,128)(2,1)} %cot.1, s32[8,64]{1,0:T(8,128)} %send_sub.1, ...), custom_call_target="tpu_custom_call" | custom-call | tf_op jit(solution)/shard_map/pallas_call | solution.py:389
  53.4 3.5 %shard_map.114 = (bf16[2048,128]{1,0:T(8,128)(2,1)}, f32[128,128]{1,0:T(8,128)}, bf16[2048,128]{1,0:T(8,128)(2,1)}) custom-call(bf16[2048,128]{1,0:T(8,128)(2,1)} %get-tuple-element.6.refs_0_, f32[128,128]{1,0:T(8,128)} %get-tuple-element.7.refs_1_, bf16[2048,128]{1,0:T(8,128)(2,1)} %get-tuple-element.8.refs_2_), custom_call_target="tpu_custom_call" | custom-call | tf_op jit(solution)/shard_map/pallas_call | solution.py:401

commit v3 on v2

--- a/solution.py
+++ b/solution.py
@@ -39,6 +39,25 @@
 
 def wrap(i, n):
     return jnp.where(i >= n, i - n, i)
+
+
+def slot_chains(rb, nh, slots, tile_index, tile_count, out):
+    out[...] = jnp.zeros_like(out)
+    out[0:2, 0:slots] = tile_index[0]
+    lanes = out.shape[1]
+    count = tile_count[0]
+    picks = out[...]
+    u = iota((lanes, lanes), 0)
+    t = iota((lanes, lanes), 1)
+    ord_u = slot_order(u, rb, nh)
+    ord_t = slot_order(t, rb, nh)
+    for which in range(2):
+        line = jnp.broadcast_to(picks[which : which + 1, :], (lanes, lanes))
+        turned = line.T
+        prev = jnp.where((turned == line) & (ord_u < ord_t) & (u < slots), ord_u, 0)
+        last = jnp.where((turned == t) & (u < count), ord_u, 0)
+        out[2 + 2 * which : 3 + 2 * which, :] = jnp.max(prev, axis=0, keepdims=True)
+        out[3 + 2 * which : 4 + 2 * which, :] = jnp.max(last, axis=0, keepdims=True)
 
 
 class Exchange:
@@ -64,12 +83,12 @@
 
 def kernel(
     c,
-    feats, stale, weight, cot, send_sub, send_dom, meta_s, tiles_hbm,
-    hidden_hbm, wgrad_hbm, fgrad_hbm,
+    feats, stale, weight, cot, send_sub, send_dom, tile_index, tile_count, tiles_hbm,
+    hidden, wgrad, fgrad,
     st, xcols, tiles, cotv, chain, gbuf, aggv, gzv,
     ohg, ohs, ohd, sub_out, g_out, g_in, z_out, back, rsub, rz, rg_out, rg_in, rdom,
-    wp_out, wp_in, wm_out, wm_in, wa_out, wa_in, hidden, fgrad, wgrad, acc,
-    sem_in, ss, rs,
+    wp_out, wp_in, wm_out, wm_in, wa_out, wa_in, acc,
+    meta_v, meta_s, sem_in, ss, rs,
 ):
     ns, ng, nz, tile, rb, nh, slots = c.ns, c.ng, c.nz, c.tile, c.rb, c.nh, c.slots
     rows, cb, ssub, sdom = c.rows, c.cb, c.ssub, c.sdom
@@ -85,9 +104,6 @@
     feats_cp = pltpu.make_async_copy(feats, xcols.at[pl.ds(0, rb)], sem_in.at[1])
     tiles_cp = pltpu.make_async_copy(tiles_hbm, tiles, sem_in.at[2])
     cot_cp = pltpu.make_async_copy(cot, cotv, sem_in.at[3])
-    hidden_cp = pltpu.make_async_copy(hidden, hidden_hbm, sem_in.at[4])
-    fgrad_cp = pltpu.make_async_copy(fgrad, fgrad_hbm, sem_in.at[5])
-    wgrad_cp = pltpu.make_async_copy(wgrad, wgrad_hbm, sem_in.at[6])
     stale_cp.start()
     feats_cp.start()
     tiles_cp.start()
@@ -99,8 +115,9 @@
         offsets = [()]
         for axis in range(4):
             offsets = [o + (k,) for o in offsets for k in range(sizes[axis] if axis in steps else 1)]
+        offsets = sorted(offsets[1:], key=lambda o: -c.hops(o))
         group = []
-        for offset in offsets[1:]:
+        for offset in offsets:
             at = [wrap(m + o, n) if o else m for m, o, n in zip(mine, offset, sizes)]
             index = 0
             for axis in reversed(range(4)):
@@ -147,6 +164,10 @@
     if spare:
         xcols[cb - 1, spare:, :] = jnp.zeros((tile - spare, xcols.shape[2]), BF)
 
+    slot_chains(rb, nh, slots, tile_index, tile_count, meta_v)
+    meta_cp = pltpu.make_async_copy(meta_v, meta_s, sem_in.at[4])
+    meta_cp.start()
+
     out_r = iota((dom_total, ng * gpad), 0)
     in_r = iota((dom_total, ng * gpad), 1)
     oz, ogk = out_r // (ng * sdom), out_r % (ng * sdom)
@@ -171,10 +192,12 @@
         pieces = [send_sub[i : i + 1, :] for i in range(j * 128 // ssub, (j + 1) * 128 // ssub)]
         ohs[:, j * 128 : (j + 1) * 128] = one_hot(jnp.concatenate(pieces, axis=1) == node)
     ohd[...] = one_hot(jnp.concatenate([dom_t[k : k + 1, :] for k in range(sdom)], axis=1) == node)
+    meta_cp.wait()
     fs.arrived()
-    fz.arrived()
 
     for s in (*range(nh), *range(nh + rb, slots)):
+        if s == sub_total // tile:
+            fz.arrived()
         p = s + rb if s < nh else s
         block = xcols[rb + s] if s < nh else xcols[meta_s[1, s]]
         chain[p] = dot(tiles[s], block) + chain[meta_s[2, s]]
@@ -202,7 +225,6 @@
     me_p = me_l * ns + me_s
     w1 = Exchange(by_piece, lambda p: wp_out.at[p], wp_in.at[me_p], wp_in.at[pl.ds(0, pieces - 1)], ss.at[3], rs.at[3])
     w1.start()
-    hidden_cp.start()
     wp_in[pl.ds(me_p, 1)] = wp_out[pl.ds(me_p, 1)]
 
     for s in range(slots):
@@ -265,7 +287,6 @@
     for b in range(rb // step):
         lo, hi = b * step * tile, (b + 1) * step * tile
         fgrad[lo:hi, :] = (acc[lo:hi, :] + dot(ohd[lo:hi, :], rdom[...])).astype(BF)
-    fgrad_cp.start()
 
     w2.arrived()
     piece = wm_in[0]
@@ -278,42 +299,27 @@
     wa_in[pl.ds(me_p, 1)] = piece[None]
     for x in (fg, fs, fz, bz, bs, bg, w1, w2):
         x.left()
-    hidden_cp.wait()
-    fgrad_cp.wait()
     w3.arrived()
     for i in range(pieces):
         wgrad[i * rp : (i + 1) * rp, :] = wa_in[i]
-    wgrad_cp.start()
     w3.left()
-    wgrad_cp.wait()
-
-
-def hand_over(*refs):
-    for src, dst in zip(refs[:3], refs[3:]):
-        dst[...] = src[...]
-
-
-def slot_chains(rb, nh, slots, tile_index, tile_count, out):
-    out[...] = jnp.zeros_like(out)
-    out[0:2, 0:slots] = tile_index[0]
-    lanes = out.shape[1]
-    count = tile_count[0]
-    picks = out[...]
-    u = iota((lanes, lanes), 0)
-    t = iota((lanes, lanes), 1)
-    ord_u = slot_order(u, rb, nh)
-    ord_t = slot_order(t, rb, nh)
-    for which in range(2):
-        line = jnp.broadcast_to(picks[which : which + 1, :], (lanes, lanes))
-        turned = line.T
-        prev = jnp.where((turned == line) & (ord_u < ord_t) & (u < slots), ord_u, 0)
-        last = jnp.where((turned == t) & (u < count), ord_u, 0)
-        out[2 + 2 * which : 3 + 2 * which, :] = jnp.max(prev, axis=0, keepdims=True)
-        out[3 + 2 * which : 4 + 2 * which, :] = jnp.max(last, axis=0, keepdims=True)
+
+
+def hand_over(hidden, wgrad, fgrad, *rest):
+    outs, sems = rest[:3], rest[3]
+    copies = [
+        pltpu.make_async_copy(src, dst, sems.at[i]) for i, (src, dst) in enumerate(zip((hidden, wgrad, fgrad), outs))
+    ]
+    for copy in copies:
+        copy.start()
+    for copy in copies:
+        copy.wait()
 
 
 class Sizes:
-    pass
+    def hops(self, offset):
+        s, l, h, z = offset
+        return min(s, self.ns - s) + l // 2 + 0.25 * (l % 2) + 2 * h + min(z, self.nz - z)
 
 
 def on_device(feats, stale, weight, cot, send_sub, send_dom, tile_index, tile_count, tiles):
@@ -339,12 +345,6 @@
     vmem = pl.BlockSpec(memory_space=pltpu.VMEM)
     smem = pl.BlockSpec(memory_space=pltpu.SMEM)
     hbm = pl.BlockSpec(memory_space=pltpu.HBM)
-    meta = pl.pallas_call(
-        functools.partial(slot_chains, c.rb, c.nh, c.slots),
-        out_shape=jax.ShapeDtypeStruct((8, 128), I32),
-        in_specs=[vmem, smem],
-        out_specs=vmem,
-    )(tile_index, tile_count)
     scratch = [
         pltpu.VMEM((c.rows, f), BF),
         pltpu.VMEM((c.cb, c.tile, f), BF),
@@ -373,11 +373,10 @@
         pltpu.VMEM((rest, rp, hid), F32),
         pltpu.VMEM((rp, hid), F32),
         pltpu.VMEM((pieces, rp, hid), F32),
-        pltpu.VMEM((c.rows, hid), BF),
-        pltpu.VMEM((c.rows, f), BF),
-        pltpu.VMEM((f, hid), F32),
         pltpu.VMEM((c.rows, f), F32),
-        pltpu.SemaphoreType.DMA((7,)),
+        pltpu.VMEM((8, 128), I32),
+        pltpu.SMEM((8, 128), I32),
+        pltpu.SemaphoreType.DMA((5,)),
         pltpu.SemaphoreType.DMA((9,)),
         pltpu.SemaphoreType.DMA((9,)),
     ]
@@ -388,22 +387,21 @@
     )
     results = pl.pallas_call(
         functools.partial(kernel, c),
-        out_shape=outs,
-        in_specs=[hbm, hbm, vmem, hbm, vmem, vmem, smem, hbm],
-        out_specs=(hbm, hbm, hbm),
+        out_shape=tuple(pltpu.VMEM(o.shape, o.dtype) for o in outs),
+        in_specs=[hbm, hbm, vmem, hbm, vmem, vmem, vmem, smem, hbm],
+        out_specs=(vmem, vmem, vmem),
         scratch_shapes=scratch,
         compiler_params=pltpu.CompilerParams(
-            collective_id=0, has_side_effects=True, vmem_limit_bytes=63 * 1024 * 1024
+            collective_id=0, has_side_effects=True, vmem_limit_bytes=62500 * 1024
         ),
-    )(feats.reshape(c.rb, c.tile, f), stale, weight, cot, send_sub, send_dom.T, meta, tiles)
-    steps = 4
-    blocks = [pl.BlockSpec((o.shape[0] // steps, o.shape[1]), lambda i: (i, 0)) for o in outs]
+    )(feats.reshape(c.rb, c.tile, f), stale, weight, cot, send_sub, send_dom.T, tile_index, tile_count, tiles)
     return pl.pallas_call(
         hand_over,
         out_shape=outs,
-        grid=(steps,),
-        in_specs=blocks,
-        out_specs=blocks,
+        in_specs=[vmem] * 3,
+        out_specs=(hbm,) * 3,
+        scratch_shapes=[pltpu.SemaphoreType.DMA((3,))],
+        compiler_params=pltpu.CompilerParams(vmem_limit_bytes=2 * 1024 * 1024),
     )(*results)
 
 

time: 57.2 us -> 50.5 us (0.88)
  Pallas kernels: 55.6 us -> 49 us
    pallas_call x3 -> x2, Pallas kernels: 55.6 us -> 49 us  [the longest x1 48 us: on_device(): pl.pallas_call(functools.partial(kernel, c), out_shape=tuple((pltpu.VMEM(...]
where the time goes in v3:
time: 50.5 us; the launch traced here: 50.3 us
  Pallas kernels  49 us (97%)
  between operations  1.29 us (3%)
    pallas_call x1, Pallas kernels, on_device(): pl.pallas_call(functools.partial(kernel, c), out_shape=tuple((pltpu.VMEM(...  48 us
    pallas_call x1, Pallas kernels, on_device(): pl.pallas_call(hand_over, out_shape=outs, in_specs=[vmem] * 3, out_specs=...  1.02 us

profile of v3, /device:TPU:1, one launch (start us, length us, event | category | flops | bytes accessed | tf_op | source)
XLA Modules:
  0.0 50.3 jit_solution(274704788677940925)
XLA Ops:
  1.3 48.0 %shard_map.112 = (bf16[2048,128]{1,0:T(8,128)(2,1)S(1)}, f32[128,128]{1,0:T(8,128)S(1)}, bf16[2048,128]{1,0:T(8,128)(2,1)S(1)}) custom-call(bf16[16,128,128]{2,1,0:T(8,128)(2,1)} %bitcast.2, bf16[2048,128]{1,0:T(8,128)(2,1)} %stale.1, bf16[128,128]{1,0:T(8,128)(2,1)} %weight.1, bf16[2048,128]{1,0:T(8,128)(2,1)} %cot.1, s32[8,64]{1,0:T(8,128)} %send_sub.1, ...), custom_call_target="tpu_custom_call" | custom-call | tf_op jit(solution)/shard_map/pallas_call | solution.py:388
  49.3 1.0 %shard_map.113 = (bf16[2048,128]{1,0:T(8,128)(2,1)}, f32[128,128]{1,0:T(8,128)}, bf16[2048,128]{1,0:T(8,128)(2,1)}) custom-call(bf16[2048,128]{1,0:T(8,128)(2,1)S(1)} %get-tuple-element.6.hidden, f32[128,128]{1,0:T(8,128)S(1)} %get-tuple-element.7.wgrad, bf16[2048,128]{1,0:T(8,128)(2,1)S(1)} %get-tuple-element.8.fgrad), custom_call_target="tpu_custom_call" | custom-call | tf_op jit(solution)/shard_map/pallas_call | solution.py:398

commit v4 on v3

--- a/solution.py
+++ b/solution.py
@@ -83,12 +83,12 @@
 
 def kernel(
     c,
-    feats, stale, weight, cot, send_sub, send_dom, tile_index, tile_count, tiles_hbm,
+    feats, stale, weight_hbm, cot, sub_hbm, dom_hbm, index_hbm, count_hbm, tiles_hbm,
     hidden, wgrad, fgrad,
     st, xcols, tiles, cotv, chain, gbuf, aggv, gzv,
     ohg, ohs, ohd, sub_out, g_out, g_in, z_out, back, rsub, rz, rg_out, rg_in, rdom,
     wp_out, wp_in, wm_out, wm_in, wa_out, wa_in, acc,
-    meta_v, meta_s, sem_in, ss, rs,
+    meta_v, meta_s, weight, send_sub, send_dom, tile_index, tile_count, sem_in, ss, rs,
 ):
     ns, ng, nz, tile, rb, nh, slots = c.ns, c.ng, c.nz, c.tile, c.rb, c.nh, c.slots
     rows, cb, ssub, sdom = c.rows, c.cb, c.ssub, c.sdom
@@ -104,7 +104,17 @@
     feats_cp = pltpu.make_async_copy(feats, xcols.at[pl.ds(0, rb)], sem_in.at[1])
     tiles_cp = pltpu.make_async_copy(tiles_hbm, tiles, sem_in.at[2])
     cot_cp = pltpu.make_async_copy(cot, cotv, sem_in.at[3])
+    dom_cp = pltpu.make_async_copy(dom_hbm, send_dom, sem_in.at[5])
+    sub_cp = pltpu.make_async_copy(sub_hbm, send_sub, sem_in.at[6])
+    index_cp = pltpu.make_async_copy(index_hbm, tile_index, sem_in.at[7])
+    count_cp = pltpu.make_async_copy(count_hbm, tile_count, sem_in.at[8])
+    weight_cp = pltpu.make_async_copy(weight_hbm, weight, sem_in.at[9])
+    dom_cp.start()
     stale_cp.start()
+    sub_cp.start()
+    index_cp.start()
+    count_cp.start()
+    weight_cp.start()
     feats_cp.start()
     tiles_cp.start()
     cot_cp.start()
@@ -134,6 +144,7 @@
         pl.semaphore_signal(barrier, inc=1, device_id=device, device_id_type=MESH)
 
     lane_n = iota((1, rows), 1)
+    dom_cp.wait()
     dom_t = send_dom[...]
     dom_i = jnp.transpose(jnp.concatenate([dom_t, jnp.zeros((sdom, 128 - nd), I32)], axis=1))[:nd]
     for k in range(sdom):
@@ -151,6 +162,7 @@
     fg.start()
     g_in[pl.ds(me_g, 1)] = g_out[pl.ds(me_g, 1)]
 
+    sub_cp.wait()
     sub_t = jnp.transpose(jnp.concatenate([send_sub[...], jnp.zeros((ns, 128 - ssub), I32)], axis=1))
     for j in range(ns):
         ohg[j * ssub : (j + 1) * ssub, :] = one_hot(sub_t[:ssub, j : j + 1] == lane_n)
@@ -164,6 +176,8 @@
     if spare:
         xcols[cb - 1, spare:, :] = jnp.zeros((tile - spare, xcols.shape[2]), BF)
 
+    index_cp.wait()
+    count_cp.wait()
     slot_chains(rb, nh, slots, tile_index, tile_count, meta_v)
     meta_cp = pltpu.make_async_copy(meta_v, meta_s, sem_in.at[4])
     meta_cp.start()
@@ -187,6 +201,7 @@
     for p in range(rb):
         chain[p] = dot(tiles[nh + p], xcols[p])
     cot_cp.wait()
+    weight_cp.wait()
     node = iota((rows, 1), 0)
     for j in range(sub_total // 128):
         pieces = [send_sub[i : i + 1, :] for i in range(j * 128 // ssub, (j + 1) * 128 // ssub)]
@@ -204,7 +219,6 @@
 
     step = c.step
     w = weight[...]
-    part = None
     for b in range(rb // step):
         lo, hi = b * step * tile, (b + 1) * step * tile
         for r in range(b * step, (b + 1) * step):
@@ -215,7 +229,6 @@
         hidden[lo:hi, :] = (pre * sig).astype(BF)
         gz = (cotv[lo:hi, :].astype(F32) * sig * (1.0 + pre * (1.0 - sig))).astype(BF)
         gzv[lo:hi, :] = gz
-        gbuf[b * step : (b + 1) * step] = dot_nt(gz, w).astype(BF).reshape(step, tile, -1)
     part = dot_tn(aggv[...], gzv[...])
     pieces = wp_out.shape[0]
     rp = wp_out.shape[1]
@@ -227,6 +240,9 @@
     w1.start()
     wp_in[pl.ds(me_p, 1)] = wp_out[pl.ds(me_p, 1)]
 
+    for b in range(rb // step):
+        gz = gzv[b * step * tile : (b + 1) * step * tile, :]
+        gbuf[b * step : (b + 1) * step] = dot_nt(gz, w).astype(BF).reshape(step, tile, -1)
     for s in range(slots):
         p = s + rb if s < nh else (s - nh if s < nh + rb else s)
         block = gbuf[s - nh] if nh <= s < nh + rb else gbuf[meta_s[0, s]]
@@ -277,6 +293,16 @@
         for r in range(step):
             acc[lo + r * tile : lo + (r + 1) * tile, :] = chain[meta_s[5, b * step + r]] + got[r * tile : (r + 1) * tile, :]
 
+    w2.arrived()
+    piece = wm_in[0]
+    for i in range(1, rest):
+        piece = piece + wm_in[i]
+    piece = piece * c.scale
+    wa_out[...] = piece
+    w3 = Exchange(by_piece, lambda p: wa_out, wa_in.at[me_p], wa_in.at[pl.ds(0, pieces - 1)], ss.at[8], rs.at[8])
+    w3.start()
+    wa_in[pl.ds(me_p, 1)] = piece[None]
+
     out_r = iota((dom_total, ng * gpad), 0)
     in_r = iota((dom_total, ng * gpad), 1)
     ok, ozg = out_r // nd, out_r % nd
@@ -288,15 +314,6 @@
         lo, hi = b * step * tile, (b + 1) * step * tile
         fgrad[lo:hi, :] = (acc[lo:hi, :] + dot(ohd[lo:hi, :], rdom[...])).astype(BF)
 
-    w2.arrived()
-    piece = wm_in[0]
-    for i in range(1, rest):
-        piece = piece + wm_in[i]
-    piece = piece * c.scale
-    wa_out[...] = piece
-    w3 = Exchange(by_piece, lambda p: wa_out, wa_in.at[me_p], wa_in.at[pl.ds(0, pieces - 1)], ss.at[8], rs.at[8])
-    w3.start()
-    wa_in[pl.ds(me_p, 1)] = piece[None]
     for x in (fg, fs, fz, bz, bs, bg, w1, w2):
         x.left()
     w3.arrived()
@@ -343,7 +360,6 @@
     pieces, rest = c.ns * c.nl, c.ng // c.nl * c.nz
     rp = f // pieces
     vmem = pl.BlockSpec(memory_space=pltpu.VMEM)
-    smem = pl.BlockSpec(memory_space=pltpu.SMEM)
     hbm = pl.BlockSpec(memory_space=pltpu.HBM)
     scratch = [
         pltpu.VMEM((c.rows, f), BF),
@@ -376,7 +392,12 @@
         pltpu.VMEM((c.rows, f), F32),
         pltpu.VMEM((8, 128), I32),
         pltpu.SMEM((8, 128), I32),
-        pltpu.SemaphoreType.DMA((5,)),
+        pltpu.VMEM((f, hid), BF),
+        pltpu.VMEM((c.ns, c.ssub), I32),
+        pltpu.VMEM((c.sdom, nd), I32),
+        pltpu.VMEM((1, 2, c.slots), I32),
+        pltpu.SMEM((1,), I32),
+        pltpu.SemaphoreType.DMA((10,)),
         pltpu.SemaphoreType.DMA((9,)),
         pltpu.SemaphoreType.DMA((9,)),
     ]
@@ -388,7 +409,7 @@
     results = pl.pallas_call(
         functools.partial(kernel, c),
         out_shape=tuple(pltpu.VMEM(o.shape, o.dtype) for o in outs),
-        in_specs=[hbm, hbm, vmem, hbm, vmem, vmem, vmem, smem, hbm],
+        in_specs=[hbm] * 9,
         out_specs=(vmem, vmem, vmem),
         scratch_shapes=scratch,
         compiler_params=pltpu.CompilerParams(

time: 50.5 us -> 49.7 us (0.984)
  Pallas kernels: 49 us -> 48.3 us
    pallas_call x1, Pallas kernels: 48 us -> 47.3 us  [on_device(): pl.pallas_call(functools.partial(kernel, c), out_shape=tuple((pltpu.VMEM(...]
where the time goes in v4:
time: 49.7 us; the launch traced here: 49.6 us
  Pallas kernels  48.3 us (97%)
  between operations  1.29 us (3%)
    pallas_call x1, Pallas kernels, on_device(): pl.pallas_call(functools.partial(kernel, c), out_shape=tuple((pltpu.VMEM(...  47.3 us
    pallas_call x1, Pallas kernels, on_device(): pl.pallas_call(hand_over, out_shape=outs, in_specs=[vmem] * 3, out_specs=...  1.02 us

profile of v4, /device:TPU:1, one launch (start us, length us, event | category | flops | bytes accessed | tf_op | source)
XLA Modules:
  0.0 49.6 jit_solution(8936998454775621989)
XLA Ops:
  1.3 47.3 %shard_map.112 = (bf16[2048,128]{1,0:T(8,128)(2,1)S(1)}, f32[128,128]{1,0:T(8,128)S(1)}, bf16[2048,128]{1,0:T(8,128)(2,1)S(1)}) custom-call(bf16[16,128,128]{2,1,0:T(8,128)(2,1)} %bitcast.2, bf16[2048,128]{1,0:T(8,128)(2,1)} %stale.1, bf16[128,128]{1,0:T(8,128)(2,1)} %weight_hbm.1, bf16[2048,128]{1,0:T(8,128)(2,1)} %cot.1, s32[8,64]{1,0:T(8,128)} %sub_hbm.1, ...), custom_call_target="tpu_custom_call" | custom-call | tf_op jit(solution)/shard_map/pallas_call | solution.py:409
  48.6 1.0 %shard_map.113 = (bf16[2048,128]{1,0:T(8,128)(2,1)}, f32[128,128]{1,0:T(8,128)}, bf16[2048,128]{1,0:T(8,128)(2,1)}) custom-call(bf16[2048,128]{1,0:T(8,128)(2,1)S(1)} %get-tuple-element.6.hidden, f32[128,128]{1,0:T(8,128)S(1)} %get-tuple-element.7.wgrad, bf16[2048,128]{1,0:T(8,128)(2,1)S(1)} %get-tuple-element.8.fgrad), custom_call_target="tpu_custom_call" | custom-call | tf_op jit(solution)/shard_map/pallas_call | solution.py:419

commit v5 on v4

--- a/solution.py
+++ b/solution.py
@@ -58,6 +58,12 @@
         last = jnp.where((turned == t) & (u < count), ord_u, 0)
         out[2 + 2 * which : 3 + 2 * which, :] = jnp.max(prev, axis=0, keepdims=True)
         out[3 + 2 * which : 4 + 2 * which, :] = jnp.max(last, axis=0, keepdims=True)
+
+
+def total(terms):
+    while len(terms) > 1:
+        terms = [a + b for a, b in zip(terms[::2], terms[1::2])] + terms[len(terms) // 2 * 2 :]
+    return terms[0]
 
 
 class Exchange:
@@ -146,17 +152,16 @@
     lane_n = iota((1, rows), 1)
     dom_cp.wait()
     dom_t = send_dom[...]
-    dom_i = jnp.transpose(jnp.concatenate([dom_t, jnp.zeros((sdom, 128 - nd), I32)], axis=1))[:nd]
-    for k in range(sdom):
-        ohg[sub_total + k * nd : sub_total + (k + 1) * nd, :] = one_hot(dom_i[:, k : k + 1] == lane_n)
-    stale_cp.wait()
-    picked = dot(ohg[sub_total:, :], st[...]).astype(BF)
+    dom_line = jnp.concatenate([dom_t[k : k + 1, :] for k in range(sdom)], axis=1)
     out_r = iota((ng * gpad, dom_total), 0)
     in_r = iota((ng * gpad, dom_total), 1)
     og, ozk = out_r // gpad, out_r % gpad
     want = (ozk % sdom) * nd + (ozk // sdom) * ng + og
-    perm = one_hot((want == in_r) & (ozk < nz * sdom))
-    g_out[...] = dot(perm, picked).astype(BF).reshape(g_out.shape)
+    hit = (want == in_r) & (ozk < nz * sdom)
+    dom_at = jnp.sum(jnp.where(hit, dom_line.astype(F32), 0.0), axis=1, keepdims=True)
+    ohg[sub_total:, :] = one_hot(dom_at == lane_n.astype(F32))
+    stale_cp.wait()
+    g_out[...] = dot(ohg[sub_total:, :], st[...]).astype(BF).reshape(g_out.shape)
     pl.semaphore_wait(barrier, ns + ng + nz - 3)
     fg = Exchange(by_g, lambda p: g_out.at[p], g_in.at[me_g], g_in.at[pl.ds(0, ng - 1)], ss.at[0], rs.at[0])
     fg.start()
@@ -206,7 +211,7 @@
     for j in range(sub_total // 128):
         pieces = [send_sub[i : i + 1, :] for i in range(j * 128 // ssub, (j + 1) * 128 // ssub)]
         ohs[:, j * 128 : (j + 1) * 128] = one_hot(jnp.concatenate(pieces, axis=1) == node)
-    ohd[...] = one_hot(jnp.concatenate([dom_t[k : k + 1, :] for k in range(sdom)], axis=1) == node)
+    ohd[...] = one_hot(dom_line == node)
     meta_cp.wait()
     fs.arrived()
 
@@ -226,7 +231,6 @@
         agg = aggv[lo:hi, :]
         pre = dot(agg, w)
         sig = jax.nn.sigmoid(pre)
-        hidden[lo:hi, :] = (pre * sig).astype(BF)
         gz = (cotv[lo:hi, :].astype(F32) * sig * (1.0 + pre * (1.0 - sig))).astype(BF)
         gzv[lo:hi, :] = gz
     part = dot_tn(aggv[...], gzv[...])
@@ -270,9 +274,7 @@
     turn_g = one_hot((want == in_r) & (ozk < nz * sdom))
 
     w1.arrived()
-    piece = wp_in[0]
-    for i in range(1, pieces):
-        piece = piece + wp_in[i]
+    piece = total([wp_in[i] for i in range(pieces)])
     wm_out[...] = piece
     rest = wm_in.shape[0]
     me_r = me_z * (ng // nl) + me_h
@@ -286,6 +288,11 @@
     bg.start()
     rg_in[pl.ds(me_g, 1)] = rg_out[pl.ds(me_g, 1)]
 
+    for b in range(rb // step):
+        lo, hi = b * step * tile, (b + 1) * step * tile
+        pre = dot(aggv[lo:hi, :], w)
+        hidden[lo:hi, :] = (pre * jax.nn.sigmoid(pre)).astype(BF)
+
     bs.arrived()
     for b in range(rb // step):
         lo, hi = b * step * tile, (b + 1) * step * tile
@@ -294,10 +301,7 @@
             acc[lo + r * tile : lo + (r + 1) * tile, :] = chain[meta_s[5, b * step + r]] + got[r * tile : (r + 1) * tile, :]
 
     w2.arrived()
-    piece = wm_in[0]
-    for i in range(1, rest):
-        piece = piece + wm_in[i]
-    piece = piece * c.scale
+    piece = total([wm_in[i] for i in range(rest)]) * c.scale
     wa_out[...] = piece
     w3 = Exchange(by_piece, lambda p: wa_out, wa_in.at[me_p], wa_in.at[pl.ds(0, pieces - 1)], ss.at[8], rs.at[8])
     w3.start()
@@ -352,7 +356,7 @@
     c.nh = -(-halo // c.tile)
     c.cb = c.rb + c.nh
     c.gpad = -(-c.nz * c.sdom // 16) * 16
-    c.step = max(1, c.rb // 4)
+    c.step = max(1, c.rb // 2)
     c.scale = float(1.0 / (c.rows * nd * c.ns) ** 0.5)
     hid = weight.shape[1]
     sub_total, dom_total = c.ns * c.ssub, nd * c.sdom
@@ -370,7 +374,7 @@
         pltpu.VMEM((c.rb, c.tile, f), BF),
         pltpu.VMEM((c.rows, f), BF),
         pltpu.VMEM((c.rows, hid), BF),
-        pltpu.VMEM((sub_total + dom_total, c.rows), BF),
+        pltpu.VMEM((sub_total + c.ng * c.gpad, c.rows), BF),
         pltpu.VMEM((c.rows, sub_total), BF),
         pltpu.VMEM((c.rows, dom_total), BF),
         pltpu.VMEM((c.ns, c.ssub, f), BF),

time: 49.7 us -> 49.6 us (level)
  no operation moved by 1% of the time
where the time goes in v5:
time: 49.6 us; the launch traced here: 49.5 us
  Pallas kernels  48.2 us (97%)
  between operations  1.29 us (3%)
    pallas_call x1, Pallas kernels, on_device(): pl.pallas_call(functools.partial(kernel, c), out_shape=tuple((pltpu.VMEM(...  47.2 us
    pallas_call x1, Pallas kernels, on_device(): pl.pallas_call(hand_over, out_shape=outs, in_specs=[vmem] * 3, out_specs=...  1.02 us

profile of v5, /device:TPU:1, one launch (start us, length us, event | category | flops | bytes accessed | tf_op | source)
XLA Modules:
  0.0 49.5 jit_solution(9312928285958381865)
XLA Ops:
  1.3 47.2 %shard_map.112 = (bf16[2048,128]{1,0:T(8,128)(2,1)S(1)}, f32[128,128]{1,0:T(8,128)S(1)}, bf16[2048,128]{1,0:T(8,128)(2,1)S(1)}) custom-call(bf16[16,128,128]{2,1,0:T(8,128)(2,1)} %bitcast.2, bf16[2048,128]{1,0:T(8,128)(2,1)} %stale.1, bf16[128,128]{1,0:T(8,128)(2,1)} %weight_hbm.1, bf16[2048,128]{1,0:T(8,128)(2,1)} %cot.1, s32[8,64]{1,0:T(8,128)} %sub_hbm.1, ...), custom_call_target="tpu_custom_call" | custom-call | tf_op jit(solution)/shard_map/pallas_call | solution.py:413
  48.4 1.0 %shard_map.113 = (bf16[2048,128]{1,0:T(8,128)(2,1)}, f32[128,128]{1,0:T(8,128)}, bf16[2048,128]{1,0:T(8,128)(2,1)}) custom-call(bf16[2048,128]{1,0:T(8,128)(2,1)S(1)} %get-tuple-element.6.hidden, f32[128,128]{1,0:T(8,128)S(1)} %get-tuple-element.7.wgrad, bf16[2048,128]{1,0:T(8,128)(2,1)S(1)} %get-tuple-element.8.fgrad), custom_call_target="tpu_custom_call" | custom-call | tf_op jit(solution)/shard_map/pallas_call | solution.py:423

commit v6 on v5

--- a/solution.py
+++ b/solution.py
@@ -356,7 +356,7 @@
     c.nh = -(-halo // c.tile)
     c.cb = c.rb + c.nh
     c.gpad = -(-c.nz * c.sdom // 16) * 16
-    c.step = max(1, c.rb // 2)
+    c.step = c.rb
     c.scale = float(1.0 / (c.rows * nd * c.ns) ** 0.5)
     hid = weight.shape[1]
     sub_total, dom_total = c.ns * c.ssub, nd * c.sdom

time: 49.6 us -> 50.1 us (1.010)
  no operation moved by 1% of the time
where the time goes in v6:
time: 50.1 us; the launch traced here: 49.9 us
  Pallas kernels  48.6 us (97%)
  between operations  1.29 us (3%)
    pallas_call x1, Pallas kernels, on_device(): pl.pallas_call(functools.partial(kernel, c), out_shape=tuple((pltpu.VMEM(...  47.6 us
    pallas_call x1, Pallas kernels, on_device(): pl.pallas_call(hand_over, out_shape=outs, in_specs=[vmem] * 3, out_specs=...  1.02 us

profile of v6, /device:TPU:1, one launch (start us, length us, event | category | flops | bytes accessed | tf_op | source)
XLA Modules:
  0.0 49.9 jit_solution(1120188004156210465)
XLA Ops:
  1.3 47.6 %shard_map.112 = (bf16[2048,128]{1,0:T(8,128)(2,1)S(1)}, f32[128,128]{1,0:T(8,128)S(1)}, bf16[2048,128]{1,0:T(8,128)(2,1)S(1)}) custom-call(bf16[16,128,128]{2,1,0:T(8,128)(2,1)} %bitcast.2, bf16[2048,128]{1,0:T(8,128)(2,1)} %stale.1, bf16[128,128]{1,0:T(8,128)(2,1)} %weight_hbm.1, bf16[2048,128]{1,0:T(8,128)(2,1)} %cot.1, s32[8,64]{1,0:T(8,128)} %sub_hbm.1, ...), custom_call_target="tpu_custom_call" | custom-call | tf_op jit(solution)/shard_map/pallas_call | solution.py:413
  48.9 1.0 %shard_map.113 = (bf16[2048,128]{1,0:T(8,128)(2,1)}, f32[128,128]{1,0:T(8,128)}, bf16[2048,128]{1,0:T(8,128)(2,1)}) custom-call(bf16[2048,128]{1,0:T(8,128)(2,1)S(1)} %get-tuple-element.6.hidden, f32[128,128]{1,0:T(8,128)S(1)} %get-tuple-element.7.wgrad, bf16[2048,128]{1,0:T(8,128)(2,1)S(1)} %get-tuple-element.8.fgrad), custom_call_target="tpu_custom_call" | custom-call | tf_op jit(solution)/shard_map/pallas_call | solution.py:423
